TPU v7x, 32 devices: a whole 2x2x4 slice. The times are simulated.
32 devices in a mesh: req: 8 (over z, y), tp: 4 (over x, core).
Axes of the slice: x: 2, y: 2, z: 4, core: 2. Of those that a mesh axis runs over, the one named last changes fastest.
Arguments:
- states: bfloat16 [16, 512, 1024], P('req', 'tp'), may hold values from -45 to 45
- lengths: int32 [16], P('req'), may hold values from 3 to 512, as said below
- w_qkv: bfloat16 [1024, 3, 1024], P(None, None, 'tp'), may hold values from -0.1875 to 0.1875
- b_qkv: float32 [3, 1024], P(None, 'tp'), may hold values from -3 to 3
- w_out: bfloat16 [1024, 1024], P('tp'), may hold values from -0.1875 to 0.1875
- b_out: float32 [1024], replicated, may hold values from -3 to 3
- ln1_gain: float32 [1024], replicated, may hold values from 0.1 to 1.9
- ln1_shift: float32 [1024], replicated, may hold values from -3 to 3
- w_up: bfloat16 [1024, 4096], P(None, 'tp'), may hold values from -0.1875 to 0.1875
- b_up: float32 [4096], P('tp'), may hold values from -3 to 3
- w_down: bfloat16 [4096, 1024], P('tp'), may hold values from -0.09375 to 0.09375
- b_down: float32 [1024], replicated, may hold values from -3 to 3
- ln2_gain: float32 [1024], replicated, may hold values from 0.1 to 1.9
- ln2_shift: float32 [1024], replicated, may hold values from -3 to 3
- index_rows: bfloat16 [131072, 1024], P(('req', 'tp')), may hold values from -0.1875 to 0.1875
- cand_ids: int32 [16, 64], P('req', 'tp'), may hold values from 0 to 131071
Outputs:
- hidden_out: bfloat16 [16, 512, 1024], P('req', 'tp')
- scores: float32 [16, 64], P('req', 'tp')
Inputs may be any that keep to these rules, and one draw needn't show every extreme that they name: Valid positions are the first lengths ones of a text; in every draw some text has 512.
All inputs are finite; a program needn't handle non-finite values.
Results may differ from a plain program's by a relative error of at most 0.015.
Values may be sent and summed in bfloat16 or wider, within the bound.
No kernel may reach another device: no remote copies, remote signals or barrier semaphores. Data moves between devices by JAX's collectives and lax.ppermute only.
A program may use at most 128 MiB of HBM per device.

v0:
```python
import functools

import jax
import jax.numpy as jnp
from jax import lax
from jax.experimental import pallas as pl
from jax.experimental.pallas import tpu as pltpu
from jax.sharding import PartitionSpec as P

HEAD_DIM = 64
WINDOW = 512
SLOTS = 16
BF16 = jnp.bfloat16
F32 = jnp.float32
I32 = jnp.int32
MIB = 1024 * 1024
NO_COST = pl.CostEstimate(flops=1, bytes_accessed=1, transcendentals=0)


def cost(gflop):
    return pl.CostEstimate(flops=int(gflop * 10**9) + 1, bytes_accessed=MIB, transcendentals=0)


layer_eps = 1e-05
norm_eps = 1e-06

VMEM = pl.BlockSpec(memory_space=pltpu.VMEM)
SMEM = pl.BlockSpec(memory_space=pltpu.SMEM)
HBM = pl.BlockSpec(memory_space=pltpu.HBM)
ANY = pl.BlockSpec(memory_space=pl.ANY)


def layer_norm(values, gain, shift):
    centre = values - jnp.mean(values, axis=-1, keepdims=True)
    spread = jnp.mean(centre * centre, axis=-1, keepdims=True)
    return centre * lax.rsqrt(spread + layer_eps) * gain + shift


def in_hbm(array):
    return pltpu.with_memory_space_constraint(array, pltpu.HBM)


def swap(value, axis, mask):
    count = lax.axis_size(axis)
    return lax.ppermute(value, axis, [(i, i ^ mask) for i in range(count)])


def matmul(left, right):
    return jnp.dot(left, right, preferred_element_type=F32)


def params(mib):
    return pltpu.CompilerParams(vmem_limit_bytes=mib * MIB)


def after(value, *others):
    return lax.optimization_barrier((value,) + others)[0]


def half_kernel(w_out, half, sem):
    part = half.shape[0]
    first = pl.multiple_of((lax.axis_index("req") & 1) * part, part)
    copy = pltpu.make_async_copy(w_out.at[pl.ds(first, part)], half, sem)
    copy.start()
    copy.wait()


def half_of(w_out):
    return pl.pallas_call(
        half_kernel,
        out_shape=jax.ShapeDtypeStruct((w_out.shape[0] // 2, w_out.shape[1]), BF16),
        in_specs=[HBM],
        out_specs=VMEM,
        scratch_shapes=[pltpu.SemaphoreType.DMA],
        compiler_params=params(4),
        cost_estimate=NO_COST,
        name="half_of",
    )(in_hbm(w_out))


def first_attention_kernel(
    lengths, s0, s1, s2, s3, w, b, out, text, own, weights, parts, bias, sems
):
    core = lax.axis_index("tp") & 1
    copies = [pltpu.make_async_copy(s0.at[core], own, sems.at[3])]
    copies += [pltpu.make_async_copy(w.at[k], weights.at[k], sems.at[k]) for k in range(3)]
    for copy in copies:
        copy.start()
    copies[0].wait()
    text[...] = jnp.concatenate([own[...], s1[core], s2[core], s3[core]])
    for which in range(3):
        copies[1 + which].wait()
        project(which, text, weights, b, parts)
    attend(lengths, parts, bias, out)


def second_attention_kernel(
    rows_here, lengths, text, w, b, i0, i1, i2, i3, out, numbers, place, rounds, parts, bias
):
    plan_rows(0, rows_here, (i0, i1, i2, i3), numbers, place, rounds)
    for which in range(3):
        project(which, text, w, b, parts)
    attend(lengths, parts, bias, out)


def project(which, text, w, b, parts):
    parts[which] = (matmul(text[...], w[which]) + b[which : which + 1, :]).astype(BF16)


def attend(lengths, parts, bias, out):
    rank = lax.axis_index("tp")
    length = lengths[rank & 1]
    _, seq_len, wide = parts.shape
    share = seq_len // 4

    def position(index):
        return ((index // share) ^ rank) * share + index % share

    row_pos = position(lax.broadcasted_iota(I32, (seq_len, 1), 0))
    col_pos = position(lax.broadcasted_iota(I32, (1, seq_len), 1))
    keep = (jnp.abs(row_pos - col_pos) <= WINDOW // 2) & (col_pos < length)
    bias[...] = jnp.where(keep, F32(0.0), F32(-1e30))
    ones = jnp.ones((seq_len, 128), BF16)
    low = lax.broadcasted_iota(I32, (1, 128), 1) < HEAD_DIM
    scale = jnp.asarray(HEAD_DIM**-0.5, BF16)
    for pair in range(wide // 128):
        lanes = slice(pair * 128, (pair + 1) * 128)
        k_pair = parts[1, :, lanes]
        v_ones = jnp.concatenate([parts[2, :, lanes], ones], axis=1)
        for block in range(4):
            rows = slice(block * share, (block + 1) * share)
            q_pair = parts[0, rows, lanes] * scale
            found = []
            for head in range(2):
                chosen = low if head == 0 else jnp.logical_not(low)
                q_head = jnp.where(chosen, q_pair, jnp.zeros((), BF16))
                logits = lax.dot_general(
                    q_head, k_pair, (((1,), (1,)), ((), ())), preferred_element_type=F32
                )
                logits = logits + bias[rows, :]
                top = jnp.max(logits, axis=-1, keepdims=True)
                expo = jnp.exp(logits - top).astype(BF16)
                summed = matmul(expo, v_ones)
                found.append(summed[:, :128] / summed[:, 128:])
            context = jnp.where(low, found[0], found[1])
            context = jnp.where(row_pos[rows] < length, context, F32(0.0))
            out[rows, lanes] = context.astype(BF16)


def attention_scratch(seq_len, wide):
    return [pltpu.VMEM((3, seq_len, wide), BF16), pltpu.VMEM((seq_len, seq_len), F32)]


def first_attention(lengths, blocks, w, b):
    _, share, width = blocks[0].shape
    wide = w.shape[2]
    return pl.pallas_call(
        first_attention_kernel,
        out_shape=(
            jax.ShapeDtypeStruct((4 * share, wide), BF16),
            jax.ShapeDtypeStruct((4 * share, width), BF16),
        ),
        in_specs=[SMEM, HBM] + [VMEM] * 3 + [HBM, VMEM],
        out_specs=(VMEM, VMEM),
        scratch_shapes=[pltpu.VMEM((share, width), BF16), pltpu.VMEM(w.shape, BF16)]
        + attention_scratch(4 * share, wide)
        + [pltpu.SemaphoreType.DMA((4,))],
        compiler_params=params(14),
        cost_estimate=NO_COST,
        name="attention_own",
    )(in_hbm(lengths), in_hbm(blocks[0]), *blocks[1:], in_hbm(w), in_hbm(b))


def second_attention(lengths, text, w, b, ids, rows_here):
    seq_len = text.shape[0]
    wide = w.shape[2]
    groups, _, each = ids[0].shape
    return pl.pallas_call(
        functools.partial(second_attention_kernel, rows_here),
        out_shape=(
            jax.ShapeDtypeStruct((seq_len, wide), BF16),
            jax.ShapeDtypeStruct((2, groups * SLOTS), I32),
            jax.ShapeDtypeStruct((groups * SLOTS, 8 * each), BF16),
            jax.ShapeDtypeStruct((1,), I32),
        ),
        in_specs=[SMEM] + [VMEM] * 7,
        out_specs=(VMEM, VMEM, VMEM, SMEM),
        scratch_shapes=attention_scratch(seq_len, wide),
        compiler_params=params(12),
        cost_estimate=cost(6),
        name="attention_partner",
    )(in_hbm(lengths), text, w, b, *ids)


def joined(first, second):
    swapped = (lax.axis_index("req") & 1) != 0
    low = jnp.where(swapped, second[...], first[...])
    high = jnp.where(swapped, first[...], second[...])
    return jnp.concatenate([low, high])


def project_first_kernel(
    text, here, there, w, half_0, half_1, b, numbers, index, out, keep, send,
    chosen, tiles, rows, sems, sem,
):
    copy = pltpu.make_async_copy(numbers, chosen, sem)
    copy.start()
    half = text.shape[0] // 2
    w_there = joined(half_0, half_1)
    copy.wait()
    finish_rows = fetch_rows(chosen, index, tiles, rows, sems)
    for number in range(2):
        span = slice(number * half, (number + 1) * half)
        other = slice((1 - number) * half, (2 - number) * half)
        total = matmul(here[span, :], w[...]) + matmul(there[other, :], w_there)
        out[span, :] = total + (text[span, :].astype(F32) + b[...])
    finish_rows(keep, send)


def project_first(text, here, there, w, halves, b_out, numbers, index_rows):
    seq_len, width = text.shape
    slots = numbers.shape[1]
    half = jax.ShapeDtypeStruct((slots // 2, width), BF16)
    return pl.pallas_call(
        project_first_kernel,
        out_shape=(jax.ShapeDtypeStruct((seq_len, width), F32), half, half),
        in_specs=[VMEM] * 8 + [HBM],
        out_specs=(VMEM, VMEM, VMEM),
        scratch_shapes=fetch_scratch(slots, width),
        compiler_params=params(12 + slots // 16),
        cost_estimate=cost(1),
        name="project_first",
    )(text, here, there, w, *halves, b_out, numbers, in_hbm(index_rows))


def project_second_kernel(base, context, w, out):
    out[...] = base[...] + matmul(context[...], w[...])


def project_second(base, context, w):
    return pl.pallas_call(
        project_second_kernel,
        out_shape=jax.ShapeDtypeStruct(base.shape, F32),
        in_specs=[VMEM] * 3,
        out_specs=VMEM,
        input_output_aliases={0: 0},
        compiler_params=params(12),
        cost_estimate=cost(1),
        name="project_second",
    )(base, context, w)


def feed_kernel(
    keep_rest, base, c3, half_0, half_1, gain, shift, b0, b1, b_down,
    up_own, up_partner, down_own, down_partner, out, up_buf, down_buf, act, sems,
):
    hidden = up_own.shape[1]
    up_copy = pltpu.make_async_copy(up_own, up_buf, sems.at[0])
    down_copy = pltpu.make_async_copy(down_own, down_buf, sems.at[1])
    up_copy.start()
    down_copy.start()
    total = base[...] + matmul(c3[...], joined(half_0, half_1))
    normed = layer_norm(total, gain[...], shift[...]).astype(BF16)
    step = 512
    for part, (weight, bias) in enumerate(((up_partner, b1), (up_buf, b0))):
        if part == 1:
            up_copy.wait()
        for low in range(0, hidden, step):
            lanes = slice(low, low + step)
            up = matmul(normed, weight[:, lanes]) + bias[:, lanes]
            activated = 0.5 * up * (1.0 + lax.erf(up * F32(0.5**0.5)))
            act[:, part * hidden + low : part * hidden + low + step] = activated.astype(BF16)
    down = matmul(act[:, :hidden], down_partner[...])
    down_copy.wait()
    down = down + matmul(act[:, hidden:], down_buf[...])
    if keep_rest:
        down = down + (normed.astype(F32) + b_down[...])
    out[...] = down.astype(out.dtype)


def feed_forward(keep_rest, base, context, halves, gain, shift, biases, b_down, ups, downs):
    seq_len, width = base.shape
    half = seq_len // 2
    here = 0 if keep_rest else 1
    hidden = ups[0].shape[1]
    heads_wide = context.shape[1]
    base_spec = pl.BlockSpec((half, width), lambda i: (here, 0))
    context_spec = pl.BlockSpec((half, heads_wide), lambda i: (1 - here, 0))
    return pl.pallas_call(
        lambda *refs: feed_kernel(keep_rest, *refs),
        out_shape=jax.ShapeDtypeStruct((half, width), F32 if keep_rest else BF16),
        grid=(1,),
        in_specs=[base_spec, context_spec] + [VMEM] * 7
        + [HBM, VMEM, HBM, VMEM],
        out_specs=VMEM,
        scratch_shapes=[
            pltpu.VMEM((width, hidden), BF16),
            pltpu.VMEM((hidden, width), BF16),
            pltpu.VMEM((half, 2 * hidden), BF16),
            pltpu.SemaphoreType.DMA((2,)),
        ],
        compiler_params=params(20),
        cost_estimate=cost(8),
        name="feed_here" if keep_rest else "feed_there",
    )(base, context, *halves, gain, shift, *biases, b_down, in_hbm(ups[0]), ups[1],
      in_hbm(downs[0]), downs[1])


def finish_kernel(lengths, here, there, gain, shift, own, other, pool):
    rank = lax.axis_index("tp")
    length = lengths[rank & 1]
    share = own.shape[0]
    total = here[...] + there[...].astype(F32)
    hidden = layer_norm(total, gain[...], shift[...]).astype(BF16)
    own[...] = hidden[:share]
    other[...] = hidden[share:]
    index = lax.broadcasted_iota(I32, (2 * share, 1), 0)
    pos = ((index // share) ^ rank) * share + index % share
    valid = jnp.where(pos < length, hidden.astype(F32), F32(0.0))
    pool[...] = jnp.sum(valid, axis=0, keepdims=True)


def finish(lengths, here, there, gain, shift):
    half, width = here.shape
    block = jax.ShapeDtypeStruct((half // 2, width), BF16)
    return pl.pallas_call(
        finish_kernel,
        out_shape=(block, block, jax.ShapeDtypeStruct((1, width), F32)),
        in_specs=[SMEM] + [VMEM] * 4,
        out_specs=(VMEM, VMEM, VMEM),
        compiler_params=params(8),
        cost_estimate=cost(2),
        name="finish",
    )(lengths, here, there, gain, shift)


def score_kernel(
    lengths, pool, pool_core, pool_chip, pool_diag, rows, own, other, out, hidden_out
):
    core = lax.axis_index("tp") & 1
    width = pool.shape[1]
    mine = pool[...] + pool_chip[...]
    theirs = pool_core[...] + pool_diag[...]
    first = jnp.where(core == 0, mine, theirs) / lengths[0].astype(F32)
    second = jnp.where(core == 0, theirs, mine) / lengths[1].astype(F32)
    row = lax.broadcasted_iota(I32, (8, width), 0)
    pooled = jnp.where(row == 0, first, jnp.where(row == 1, second, F32(0.0)))
    scale = lax.rsqrt(jnp.mean(pooled * pooled, axis=-1, keepdims=True) + norm_eps)
    queries = (pooled * scale).astype(BF16)
    found = lax.dot_general(
        queries, rows[...], (((1,), (1,)), ((), ())), preferred_element_type=F32
    )
    each = rows.shape[0] // 2
    out[0:1, :] = found[0:1, :each]
    out[1:2, :] = found[1:2, each:]
    hidden_out[core] = own[...]
    hidden_out[1 - core] = other[...]


def score(lengths, pools, rows, own, other):
    return pl.pallas_call(
        score_kernel,
        out_shape=(
            jax.ShapeDtypeStruct((2, rows.shape[0] // 2), F32),
            jax.ShapeDtypeStruct((2,) + own.shape, BF16),
        ),
        in_specs=[SMEM] + [VMEM] * 7,
        out_specs=(VMEM, VMEM),
        compiler_params=params(8),
        cost_estimate=cost(1),
        name="score",
    )(lengths, *pools, rows, own, other)


def source_order(groups):
    order = [0]
    mask = groups // 2
    while mask >= 4:
        order = order + [entry + mask for entry in order]
        mask //= 2
    return [entry + last for last in range(4) for entry in order]


def as_ones(mask):
    return mask.astype(F32).astype(BF16)


def plan_rows(first_place, rows_here, parts, numbers, place, rounds):
    rank = lax.axis_index("tp")
    group = lax.axis_index("req")
    groups = parts[0].shape[0]
    slots = groups * SLOTS
    ids = jnp.concatenate([part[:, text, :] for part in parts for text in range(2)], axis=1)
    count = ids.shape[1]
    owner = lax.shift_right_logical(ids, I32(rows_here.bit_length() - 1))
    before = as_ones(
        lax.broadcasted_iota(I32, (count, count), 0)
        < lax.broadcasted_iota(I32, (count, count), 1)
    )
    ones = jnp.ones((count, 128), BF16)
    slot = lax.broadcasted_iota(I32, (SLOTS, 1), 0) + first_place

    mine = owner == group * 4 + rank
    asked = jnp.concatenate(
        [
            (owner[:1] == (group ^ source) * 4 + rank).astype(F32)
            for source in source_order(groups)
        ]
    )
    both = jnp.concatenate([mine.astype(F32), asked]).astype(BF16)
    ranks = matmul(both, before).astype(I32)
    send_rank = jnp.where(mine, ranks[:groups], -1)
    take_rank = jnp.where(asked > 0, ranks[groups:], -1)

    local = jnp.where(mine, ids - (group * 4 + rank) * rows_here, 0)
    high = (local >> 6).astype(F32).astype(BF16)
    low = (local & 63).astype(F32).astype(BF16)
    chosen = jnp.concatenate(
        [(send_rank[k : k + 1] == slot).astype(F32) for k in range(groups)]
    ).astype(BF16)
    spread = (((1,), (1,)), ((), ()))
    wanted = 64.0 * lax.dot_general(high, chosen, spread, preferred_element_type=F32)
    wanted = wanted + lax.dot_general(low, chosen, spread, preferred_element_type=F32)
    counts = matmul(as_ones(mine), jnp.ones((count, slots), BF16))
    own = lax.broadcasted_iota(I32, (groups, slots), 0) == lax.div(
        lax.broadcasted_iota(I32, (groups, slots), 1), I32(SLOTS)
    )
    numbers[0:1, :] = jnp.sum(jnp.where(own, wanted, 0.0), axis=0, keepdims=True).astype(I32)
    counts = jnp.sum(jnp.where(own, counts, 0.0), axis=0, keepdims=True).astype(I32)
    numbers[1:2, :] = counts - first_place

    for k in range(groups):
        place[k * SLOTS : (k + 1) * SLOTS, :] = as_ones(take_rank[k : k + 1] == slot)
    shard = lax.broadcasted_iota(I32, (4 * groups, 1), 0)
    load = jnp.concatenate(
        [(owner[k : k + 1] == shard).astype(F32) for k in range(groups)]
    ).astype(BF16)
    most = jnp.max(matmul(load, ones)).astype(I32)
    rounds[0] = (most + SLOTS - 1) // SLOTS


def fetch_rows(chosen, index, tiles, rows, sems):
    deep = tiles.shape[1]
    slots = tiles.shape[0]
    step = 4

    def tile_copy(slot):
        first = pl.multiple_of((chosen[0, slot] // deep) * deep, deep)
        return pltpu.make_async_copy(index.at[pl.ds(first, deep)], tiles.at[slot], sems.at[slot])

    def start(number, carry):
        for each in range(step):
            tile_copy(number * step + each).start()
        return carry

    def select(number, carry):
        for each in range(step):
            tile_copy(number * step + each).wait()
        for each in range(step):
            source = number * step + each
            line = lax.broadcasted_iota(I32, (deep, 1), 0) == chosen[0, source] % deep
            row = jnp.where(line, tiles[source].astype(F32), F32(0.0))
            rows[pl.ds(source, 1), :] = jnp.sum(row, axis=0, keepdims=True)
        return carry

    def each_group(action):
        def one(number, carry):
            first = number * (SLOTS // step)
            left = jnp.clip(chosen[1, number * SLOTS], 0, SLOTS)
            return lax.fori_loop(first, first + (left + step - 1) // step, action, carry)

        lax.fori_loop(0, slots // SLOTS, one, 0)

    rows[...] = jnp.zeros_like(rows)
    each_group(start)

    def finish_rows(keep, send):
        each_group(select)
        keep[...] = rows[: slots // 2, :].astype(BF16)
        send[...] = rows[slots // 2 :, :].astype(BF16)

    return finish_rows


def take_kernel(
    number, i0, i1, i2, i3, index, keep, send, place, rounds, numbers, chosen, tiles, rows,
    sems, sem,
):
    plan_rows(number[0] * SLOTS, index.shape[0], (i0, i1, i2, i3), numbers, place, rounds)
    copy = pltpu.make_async_copy(numbers, chosen, sem)
    copy.start()
    copy.wait()
    fetch_rows(chosen, index, tiles, rows, sems)(keep, send)


def fetch_scratch(slots, width):
    return [
        pltpu.SMEM((2, slots), I32),
        pltpu.VMEM((slots, 16, width), BF16),
        pltpu.VMEM((slots, width), F32),
        pltpu.SemaphoreType.DMA((slots,)),
        pltpu.SemaphoreType.DMA,
    ]


def take_rows(number, ids, index_rows):
    groups, _, each = ids[0].shape
    slots = groups * SLOTS
    width = index_rows.shape[1]
    half = jax.ShapeDtypeStruct((slots // 2, width), BF16)
    return pl.pallas_call(
        take_kernel,
        out_shape=(
            half,
            half,
            jax.ShapeDtypeStruct((slots, 8 * each), BF16),
            jax.ShapeDtypeStruct((1,), I32),
        ),
        in_specs=[SMEM] + [VMEM] * 4 + [HBM],
        out_specs=(VMEM, VMEM, VMEM, SMEM),
        scratch_shapes=[pltpu.VMEM((2, slots), I32)] + fetch_scratch(slots, width),
        compiler_params=params(8 + slots // 16),
        cost_estimate=NO_COST,
        name="take_rows",
    )(number, *ids, in_hbm(index_rows))


def place_kernel(place, h0, h1, h2, h3, out):
    received = jnp.concatenate([h0[...], h1[...], h2[...], h3[...]])
    chosen = lax.dot_general(
        place[...], received, (((0,), (0,)), ((), ())), preferred_element_type=F32
    )
    out[...] = chosen.astype(BF16)


def place_rows(place, received):
    return pl.pallas_call(
        place_kernel,
        out_shape=jax.ShapeDtypeStruct((place.shape[1], received[0].shape[1]), BF16),
        in_specs=[VMEM] * 5,
        out_specs=VMEM,
        compiler_params=params(8),
        cost_estimate=NO_COST,
        name="place_rows",
    )(place, *received)


def masks(axis):
    mask = 1
    while mask < lax.axis_size(axis):
        yield mask
        mask *= 2


def row_exchange(ids, index_rows, place, rounds):
    width = index_rows.shape[1]

    def gathered(keep, send, place, gates=((), (), ())):
        keep = keep.reshape(1, -1, SLOTS, width)
        send = send.reshape(1, -1, SLOTS, width)
        held = None
        for mask in list(masks("req"))[:1:-1]:
            if held is not None:
                keep, send = held[:, :mask], held[:, mask:]
            other = swap(send, "req", mask)
            if mask == 4:
                other = after(other, *gates[0])
            held = jnp.concatenate([keep, other])
        others = [swap(held[:, mask], "req", mask) for mask in (1, 2, 3)]
        others = list(after(tuple(others), *gates[1]))
        held = [part.reshape(-1, width) for part in [held[:, 0]] + others]
        found = place_rows(place, held)
        found = after(found, *gates[2]).reshape(4, -1, width)
        parts = [swap(found[mask], "tp", mask) for mask in (1, 2, 3)]
        return found[0] + parts[0] + parts[1] + parts[2]

    def one_more(number, total):
        keep, send, place, _ = take_rows(number.reshape(1), ids, index_rows)
        return total + gathered(keep, send, place)

    def further(rows):
        return lax.fori_loop(1, rounds[0], one_more, rows)

    return lambda keep, send, *gates: gathered(keep, send, place, gates), further


def per_device(
    states,
    lengths,
    w_qkv,
    b_qkv,
    w_out,
    b_out,
    ln1_gain,
    ln1_shift,
    w_up,
    b_up,
    w_down,
    b_down,
    ln2_gain,
    ln2_shift,
    index_rows,
    cand_ids,
):
    from_chip = swap(states, "tp", 2)
    from_core = swap(states, "tp", 1)
    w_qkv_t = w_qkv.transpose(1, 0, 2)
    w_qkv_p = swap(w_qkv_t, "tp", 1)
    b_qkv_p = swap(b_qkv, "tp", 1)
    b_up_p = swap(b_up, "tp", 1)

    held = cand_ids[None]
    for mask in masks("req"):
        other = swap(held, "req", mask)
        if mask * 2 == lax.axis_size("req"):
            w_half = half_of(after(w_out, held))
            other, w_half = lax.optimization_barrier((other, w_half))
        held = jnp.concatenate([held, other])
    w_out_p = swap(w_out, "tp", 1)
    from_chip, held, from_core, w_qkv_p, b_qkv_p, b_up_p, w_out_p = lax.optimization_barrier(
        (from_chip, held, from_core, w_qkv_p, b_qkv_p, b_up_p, w_out_p)
    )
    from_diag = swap(from_chip, "tp", 1)
    blocks = (states, from_core, from_chip, from_diag)
    ids = (held,) + tuple(swap(held, "tp", mask) for mask in (1, 2, 3))
    w_up_p = swap(after(w_up, from_diag, *ids), "tp", 1)
    w_down_p = swap(after(w_down, from_diag, *ids), "tp", 1)
    w_x0 = swap(after(w_half, ids[2]), "tp", 2)

    blocks, ids = lax.optimization_barrier((blocks, ids))
    context_0, text = first_attention(lengths, blocks, w_qkv_t, b_qkv)
    context_0x = swap(context_0, "tp", 2)
    w_x1 = swap(after(w_x0, context_0), "req", 1)
    context_1, numbers, place, rounds = second_attention(
        lengths, text, w_qkv_p, b_qkv_p, ids, index_rows.shape[0]
    )
    context_1x = swap(context_1, "tp", 2)
    w_d0 = swap(after(w_x0, context_0), "tp", 1)
    w_d1 = swap(after(w_x1, context_1), "tp", 1)

    base, keep, send = project_first(
        text, context_0, context_0x, w_out, (w_x0, w_x1), b_out[None], numbers,
        index_rows,
    )
    base = project_second(base, context_1, w_out_p)
    gathered, further = row_exchange(ids, index_rows, place, rounds)
    common = (
        context_1x, (w_d0, w_d1), ln1_gain[None], ln1_shift[None],
        (b_up[None], b_up_p[None]), b_down[None], (w_up, w_up_p),
        (w_down, w_down_p),
    )
    down_there = feed_forward(False, base, *common)
    down_x = swap(down_there, "tp", 2)
    down_here = feed_forward(True, after(base, down_there), *common)
    down_x = after(down_x, down_here)
    hidden, hidden_other, pool = finish(
        lengths, down_here, down_x, ln2_gain[None], ln2_shift[None]
    )

    rows = gathered(keep, after(send, down_there), (down_here,), (down_here,), (hidden,))
    pools = (pool,) + tuple(swap(pool, "tp", mask) for mask in (1, 2, 3))
    hidden_p = swap(hidden_other, "tp", 1)
    rows = further(after(rows, *pools))
    scores, hidden_out = score(lengths, pools, rows, hidden, hidden_p)
    return (hidden_out, scores)


def solution(mesh):
    placed = (
        P("req", "tp", None),
        P("req"),
        P(None, None, "tp"),
        P(None, "tp"),
        P("tp", None),
        P(),
        P(),
        P(),
        P(None, "tp"),
        P("tp"),
        P("tp", None),
        P(),
        P(),
        P(),
        P(("req", "tp"), None),
        P("req", "tp"),
    )
    return jax.shard_map(
        per_device,
        mesh=mesh,
        in_specs=placed,
        out_specs=(P("req", "tp", None), P("req", "tp")),
        check_vma=False,
    )
```

profile of v0, /device:TPU:0, one launch (start us, length us, event | category | flops | bytes accessed | tf_op | source)
XLA Modules:
  0.0 78.8 jit_solution(6166221480683381954)
XLA Ops:
  1.1 2.6 %collective-permute-start.7 = (bf16[2,128,1024]{2,1,0:T(8,128)(2,1)}, bf16[2,128,1024]{2,1,0:T(8,128)(2,1)S(1)}, u32[]{:S(2)}, u32[]{:S(2)}) collective-permute-start(bf16[2,128,1024]{2,1,0:T(8,128)(2,1)} %s0), channel_id=1, source_target_pairs={{0,2},{1,3},{2,0},{3,1},{4,6},{5,7},{6,4},{7,5},{8,10},{9,11},{10,... | collective-permute-start | bytes 1572872 | tf_op jit(solution)/shard_map/ppermute | solution.py:45
  4.2 1.5 %collective-permute-start.8 = (s32[1,2,16]{2,1,0:T(2,128)}, s32[1,2,16]{2,1,0:T(2,128)S(1)}, u32[]{:S(2)}, u32[]{:S(2)}) collective-permute-start(s32[1,2,16]{2,1,0:T(2,128)} %bitcast.87), channel_id=1, source_target_pairs={{0,4},{4,0},{8,12},{12,8},{16,20},{20,16},{24,28},{28,24},{1,5},{5... | collective-permute-start | bytes 392 | tf_op jit(solution)/shard_map/ppermute | solution.py:45
  5.7 2.3 %collective-permute-done.8 = s32[1,2,16]{2,1,0:T(2,128)S(1)} collective-permute-done((s32[1,2,16]{2,1,0:T(2,128)}, s32[1,2,16]{2,1,0:T(2,128)S(1)}, u32[]{:S(2)}, u32[]{:S(2)}) %collective-permute-start.8) | collective-permute-done | bytes 160 | tf_op jit(solution)/shard_map/ppermute | solution.py:45
  8.7 1.6 %collective-permute-start.9 = (s32[2,2,16]{2,1,0:T(2,128)S(1)}, s32[2,2,16]{2,1,0:T(2,128)S(1)}, u32[]{:S(2)}, u32[]{:S(2)}) collective-permute-start(s32[2,2,16]{2,1,0:T(2,128)S(1)} %pad_add_fusion.2), channel_id=1, source_target_pairs={{0,8},{4,12},{8,0},{12,4},{16,24},{20,28},{24,16},{28,20},{1,9},{5... | collective-permute-start | bytes 776 | tf_op jit(solution)/shard_map/ppermute | solution.py:45
  10.3 2.0 %collective-permute-done.9 = s32[2,2,16]{2,1,0:T(2,128)S(1)} collective-permute-done((s32[2,2,16]{2,1,0:T(2,128)S(1)}, s32[2,2,16]{2,1,0:T(2,128)S(1)}, u32[]{:S(2)}, u32[]{:S(2)}) %collective-permute-start.9) | collective-permute-done | bytes 288 | tf_op jit(solution)/shard_map/ppermute | solution.py:45
  13.0 2.6 %collective-permute-start.10 = (s32[4,2,16]{2,1,0:T(2,128)S(1)}, s32[4,2,16]{2,1,0:T(2,128)S(1)}, u32[]{:S(2)}, u32[]{:S(2)}) collective-permute-start(s32[4,2,16]{2,1,0:T(2,128)S(1)} %pad_add_fusion.1), channel_id=1, source_target_pairs={{0,16},{4,20},{8,24},{12,28},{16,0},{20,4},{24,8},{28,12},{1,17},{... | collective-permute-start | bytes 1544 | tf_op jit(solution)/shard_map/ppermute | solution.py:45
  15.5 1.9 %collective-permute-done.10 = s32[4,2,16]{2,1,0:T(2,128)S(1)} collective-permute-done((s32[4,2,16]{2,1,0:T(2,128)S(1)}, s32[4,2,16]{2,1,0:T(2,128)S(1)}, u32[]{:S(2)}, u32[]{:S(2)}) %collective-permute-start.10) | collective-permute-done | bytes 544 | tf_op jit(solution)/shard_map/ppermute | solution.py:45
  22.3 2.1 %collective-permute-done.18.i2 = s32[8,2,16]{2,1,0:T(2,128)S(1)} collective-permute-done((s32[8,2,16]{2,1,0:T(2,128)S(1)}, s32[8,2,16]{2,1,0:T(2,128)S(1)}, u32[]{:S(2)}, u32[]{:S(2)}) %collective-permute-start.18) | collective-permute-done | bytes 1056 | tf_op jit(solution)/shard_map/ppermute | solution.py:45
  25.0 1.5 %collective-permute-start.21 = (bf16[128,1024]{1,0:T(8,128)(2,1)S(1)}, bf16[128,1024]{1,0:T(8,128)(2,1)S(1)}, u32[]{:S(2)}, u32[]{:S(2)}) collective-permute-start(bf16[128,1024]{1,0:T(8,128)(2,1)S(1)} %half_of.1), channel_id=1, source_target_pairs={{0,2},{1,3},{2,0},{3,1},{4,6},{5,7},{6,4},{7,5},{8,10},{9,11},{10,... | collective-permute-start | bytes 786440 | tf_op jit(solution)/shard_map/ppermute | solution.py:45
  26.4 6.1 %attention_own.1 = (bf16[512,256]{1,0:T(8,128)(2,1)S(1)}, bf16[512,1024]{1,0:T(8,128)(2,1)S(1)}) custom-call(s32[2]{0:T(128)} %lengths.7, bf16[2,128,1024]{2,1,0:T(8,128)(2,1)} %s0, bf16[2,128,1024]{2,1,0:T(8,128)(2,1)S(1)} %collective-permute-done.11.s1, bf16[2,128,1024]{2,1,0:T(8,128)(2,1)S(1)} %collective-permute-done.7.s2, ...), custom_call_target="tpu_custom_call" | custom-call | flops 1 | bytes 1 | tf_op jit(solution)/shard_map/attention_own/pallas_call | solution.py:157
  33.3 1.6 %collective-permute-start.22 = (bf16[128,1024]{1,0:T(8,128)(2,1)S(1)}, bf16[128,1024]{1,0:T(8,128)(2,1)S(1)}, u32[]{:S(2)}, u32[]{:S(2)}) collective-permute-start(bf16[128,1024]{1,0:T(8,128)(2,1)S(1)} %collective-permute-done.21.half_0), channel_id=1, source_target_pairs={{0,4},{4,0},{8,12},{12,8},{16,20},{20,16},{24,28},{28,24},{1,5},{5... | collective-permute-start | bytes 786440 | tf_op jit(solution)/shard_map/ppermute | solution.py:45
  34.9 5.0 %attention_partner.1 = (bf16[512,256]{1,0:T(8,128)(2,1)S(1)}, s32[2,128]{1,0:T(2,128)S(1)}, bf16[128,128]{1,0:T(8,128)(2,1)S(1)}, s32[1]{0:T(128)}) custom-call(s32[2]{0:T(128)} %lengths.7, bf16[512,1024]{1,0:T(8,128)(2,1)S(1)} %get-tuple-element.106.text, bf16[3,1024,256]{2,1,0:T(8,128)(2,1)S(1)} %collective-permute-done.12.w, ...), custom_call_target="tpu_custom_call" | custom-call | flops 6000000000 | bytes 1048576 | tf_op jit(solution)/shard_map/attention_partner/pallas_call | solution.py:178
  39.9 1.5 %collective-permute-start.23 = (bf16[512,256]{1,0:T(8,128)(2,1)S(1)}, bf16[512,256]{1,0:T(8,128)(2,1)S(1)}, u32[]{:S(2)}, u32[]{:S(2)}) collective-permute-start(bf16[512,256]{1,0:T(8,128)(2,1)S(1)} %get-tuple-element.119.context), channel_id=1, source_target_pairs={{0,2},{1,3},{2,0},{3,1},{4,6},{5,7},{6,4},{7,5},{8,10},{9,11},{10,... | collective-permute-start | bytes 786440 | tf_op jit(solution)/shard_map/ppermute | solution.py:45
  41.9 4.1 %project_first.1 = (f32[512,1024]{1,0:T(8,128)S(1)}, bf16[64,1024]{1,0:T(8,128)(2,1)S(1)}, bf16[64,1024]{1,0:T(8,128)(2,1)S(1)}) custom-call(bf16[512,1024]{1,0:T(8,128)(2,1)S(1)} %get-tuple-element.106.text, bf16[512,256]{1,0:T(8,128)(2,1)S(1)} %get-tuple-element.107.here, bf16[512,256]{1,0:T(8,128)(2,1)S(1)} %collective-permute-done.20.there, ...), custom_call_target="tpu_custom_call" | custom-call | flops 1000000000 | bytes 1048576 | tf_op jit(solution)/shard_map/project_first/pallas_call | solution.py:224
  47.4 3.8 %feed_there.1 = bf16[256,1024]{1,0:T(8,128)(2,1)S(1)} custom-call(f32[512,1024]{1,0:T(8,128)S(1)} %project_second.1.refs_0_, bf16[512,256]{1,0:T(8,128)(2,1)S(1)} %collective-permute-done.23.refs_1_, bf16[128,1024]{1,0:T(8,128)(2,1)S(1)} %collective-permute-done.24.refs_2_, bf16[128,1024]{1,0:T(8,128)(2,1)S(1)} %collective-permute-done.25.refs_3_, ...), custom_call_target="tpu_custom_call" | custom-call | flops 8000000000 | bytes 1048576 | tf_op jit(solution)/shard_map/feed_there/pallas_call | solution.py:289
  51.2 1.5 %collective-permute-start.28 = (bf16[256,1024]{1,0:T(8,128)(2,1)S(1)}, bf16[256,1024]{1,0:T(8,128)(2,1)S(1)}, u32[]{:S(2)}, u32[]{:S(2)}) collective-permute-start(bf16[256,1024]{1,0:T(8,128)(2,1)S(1)} %feed_there.1), channel_id=1, source_target_pairs={{0,2},{1,3},{2,0},{3,1},{4,6},{5,7},{6,4},{7,5},{8,10},{9,11},{10,... | collective-permute-start | bytes 1572872 | tf_op jit(solution)/shard_map/ppermute | solution.py:45
  52.7 2.6 %collective-permute-start.32 = (bf16[1,4,16,1024]{3,2,0,1:T(8,128)(2,1)S(1)}, bf16[1,4,16,1024]{3,2,0,1:T(8,128)(2,1)S(1)}, u32[]{:S(2)}, u32[]{:S(2)}) collective-permute-start(bf16[1,4,16,1024]{3,2,0,1:T(8,128)(2,1)S(1)} %bitcast.71), channel_id=1, source_target_pairs={{0,16},{4,20},{8,24},{12,28},{16,0},{20,4},{24,8},{28,12},{1,17},{... | collective-permute-start | bytes 393224 | tf_op jit(solution)/shard_map/ppermute | solution.py:45
  55.3 3.8 %feed_here.1.here = f32[256,1024]{1,0:T(8,128)S(1)} custom-call(f32[512,1024]{1,0:T(8,128)S(1)} %project_second.1.refs_0_, bf16[512,256]{1,0:T(8,128)(2,1)S(1)} %collective-permute-done.23.refs_1_, bf16[128,1024]{1,0:T(8,128)(2,1)S(1)} %collective-permute-done.24.refs_2_, bf16[128,1024]{1,0:T(8,128)(2,1)S(1)} %collective-permute-done.25.refs_3_, ...), custom_call_target="tpu_custom_call" | custom-call | flops 8000000000 | bytes 1048576 | tf_op jit(solution)/shard_map/feed_here/pallas_call | solution.py:289
  59.1 1.6 %collective-permute-done.32 = bf16[1,4,16,1024]{3,2,0,1:T(8,128)(2,1)S(1)} collective-permute-done((bf16[1,4,16,1024]{3,2,0,1:T(8,128)(2,1)S(1)}, bf16[1,4,16,1024]{3,2,0,1:T(8,128)(2,1)S(1)}, u32[]{:S(2)}, u32[]{:S(2)}) %collective-permute-start.32) | collective-permute-done | bytes 131104 | tf_op jit(solution)/shard_map/ppermute | solution.py:45
  60.7 1.7 %collective-permute-start.33 = (bf16[2,16,1024]{2,1,0:T(8,128)(2,1)S(1)}, bf16[2,16,1024]{2,1,0:T(8,128)(2,1)S(1)}, u32[]{:S(2)}, u32[]{:S(2)}) collective-permute-start(bf16[2,16,1024]{2,1,0:T(8,128)(2,1)S(1)} %get-tuple-element.172), channel_id=1, source_target_pairs={{0,4},{4,0},{8,12},{12,8},{16,20},{20,16},{24,28},{28,24},{1,5},{5... | collective-permute-start | bytes 196616 | tf_op jit(solution)/shard_map/ppermute | solution.py:45
  65.0 1.7 %collective-permute-done.34 = bf16[2,16,1024]{2,1,0:T(8,128)(2,1)S(1)} collective-permute-done((bf16[2,16,1024]{2,1,0:T(8,128)(2,1)S(1)}, bf16[2,16,1024]{2,1,0:T(8,128)(2,1)S(1)}, u32[]{:S(2)}, u32[]{:S(2)}) %collective-permute-start.34) | collective-permute-done | bytes 65568 | tf_op jit(solution)/shard_map/ppermute | solution.py:45
  66.7 1.5 %collective-permute-done.35 = bf16[2,16,1024]{2,1,0:T(8,128)(2,1)S(1)} collective-permute-done((bf16[2,16,1024]{2,1,0:T(8,128)(2,1)S(1)}, bf16[2,16,1024]{2,1,0:T(8,128)(2,1)S(1)}, u32[]{:S(2)}, u32[]{:S(2)}) %collective-permute-start.35) | collective-permute-done | bytes 65568 | tf_op jit(solution)/shard_map/ppermute | solution.py:45
  70.2 1.4 %collective-permute-start.36 = (bf16[32,1024]{1,0:T(8,128)(2,1)S(1)}, bf16[32,1024]{1,0:T(8,128)(2,1)S(1)}, u32[]{:S(2)}, u32[]{:S(2)}) collective-permute-start(bf16[32,1024]{1,0:T(8,128)(2,1)S(1)} %get-tuple-element.167), channel_id=1, source_target_pairs={{0,1},{1,0},{2,3},{3,2},{4,5},{5,4},{6,7},{7,6},{8,9},{9,8},{10,11... | collective-permute-start | bytes 196616 | tf_op jit(solution)/shard_map/ppermute | solution.py:45
  77.2 1.6 %score.1 = (f32[2,16]{1,0:T(2,128)}, bf16[2,128,1024]{2,1,0:T(8,128)(2,1)}) custom-call(s32[2]{0:T(128)S(1)} %copy-done.2, f32[1,1024]{1,0:T(1,128)S(1)} %get-tuple-element.127.pool, f32[1,1024]{1,0:T(1,128)S(1)} %collective-permute-done.29.pool_core, f32[1,1024]{1,0:T(1,128)S(1)} %collective-permute-done.30.pool_chip, ...), custom_call_target="tpu_custom_call" | custom-call | flops 1000000000 | bytes 1048576 | tf_op jit(solution)/shard_map/score/pallas_call | solution.py:361
  (77 shorter events, 20.4 us)
Async XLA Ops:
  0.6 19.6 %collective-permute-start.12 = (bf16[3,1024,256]{2,1,0:T(8,128)(2,1)}, bf16[3,1024,256]{2,1,0:T(8,128)(2,1)S(1)}, u32[]{:S(2)}, u32[]{:S(2)}) collective-permute-start(bf16[3,1024,256]{2,1,0:T(8,128)(2,1)} %bitcast.85), channel_id=1, source_target_pairs={{0,1},{1,0},{2,3},{3,2},{4,5},{5,4},{6,7},{7,6},{8,9},{9,8},{10,11... | collective-permute-start | bytes 4718600 | tf_op jit(solution)/shard_map/ppermute | solution.py:45
  1.1 19.1 %collective-permute-start.7 = (bf16[2,128,1024]{2,1,0:T(8,128)(2,1)}, bf16[2,128,1024]{2,1,0:T(8,128)(2,1)S(1)}, u32[]{:S(2)}, u32[]{:S(2)}) collective-permute-start(bf16[2,128,1024]{2,1,0:T(8,128)(2,1)} %s0), channel_id=1, source_target_pairs={{0,2},{1,3},{2,0},{3,1},{4,6},{5,7},{6,4},{7,5},{8,10},{9,11},{10,... | collective-permute-start | bytes 1572872 | tf_op jit(solution)/shard_map/ppermute | solution.py:45
  3.7 16.5 %collective-permute-start.11 = (bf16[2,128,1024]{2,1,0:T(8,128)(2,1)}, bf16[2,128,1024]{2,1,0:T(8,128)(2,1)S(1)}, u32[]{:S(2)}, u32[]{:S(2)}) collective-permute-start(bf16[2,128,1024]{2,1,0:T(8,128)(2,1)} %s0), channel_id=1, source_target_pairs={{0,1},{1,0},{2,3},{3,2},{4,5},{5,4},{6,7},{7,6},{8,9},{9,8},{10,11... | collective-permute-start | bytes 1572872 | tf_op jit(solution)/shard_map/ppermute | solution.py:45
  3.9 16.4 %collective-permute-start.15 = (bf16[256,1024]{1,0:T(8,128)(2,1)}, bf16[256,1024]{1,0:T(8,128)(2,1)S(1)}, u32[]{:S(2)}, u32[]{:S(2)}) collective-permute-start(bf16[256,1024]{1,0:T(8,128)(2,1)} %w.1), channel_id=1, source_target_pairs={{0,1},{1,0},{2,3},{3,2},{4,5},{5,4},{6,7},{7,6},{8,9},{9,8},{10,11... | collective-permute-start | bytes 1572872 | tf_op jit(solution)/shard_map/ppermute | solution.py:45
  4.2 3.8 %collective-permute-start.8 = (s32[1,2,16]{2,1,0:T(2,128)}, s32[1,2,16]{2,1,0:T(2,128)S(1)}, u32[]{:S(2)}, u32[]{:S(2)}) collective-permute-start(s32[1,2,16]{2,1,0:T(2,128)} %bitcast.87), channel_id=1, source_target_pairs={{0,4},{4,0},{8,12},{12,8},{16,20},{20,16},{24,28},{28,24},{1,5},{5... | collective-permute-start | bytes 392 | tf_op jit(solution)/shard_map/ppermute | solution.py:45
  13.0 4.5 %collective-permute-start.10 = (s32[4,2,16]{2,1,0:T(2,128)S(1)}, s32[4,2,16]{2,1,0:T(2,128)S(1)}, u32[]{:S(2)}, u32[]{:S(2)}) collective-permute-start(s32[4,2,16]{2,1,0:T(2,128)S(1)} %pad_add_fusion.1), channel_id=1, source_target_pairs={{0,16},{4,20},{8,24},{12,28},{16,0},{20,4},{24,8},{28,12},{1,17},{... | collective-permute-start | bytes 1544 | tf_op jit(solution)/shard_map/ppermute | solution.py:45
  20.2 4.2 %collective-permute-start.16 = (bf16[2,128,1024]{2,1,0:T(8,128)(2,1)S(1)}, bf16[2,128,1024]{2,1,0:T(8,128)(2,1)S(1)}, u32[]{:S(2)}, u32[]{:S(2)}) collective-permute-start(bf16[2,128,1024]{2,1,0:T(8,128)(2,1)S(1)} %collective-permute-done.7.s2), channel_id=1, source_target_pairs={{0,1},{1,0},{2,3},{3,2},{4,5},{5,4},{6,7},{7,6},{8,9},{9,8},{10,11... | collective-permute-start | bytes 1572872 | tf_op jit(solution)/shard_map/ppermute | solution.py:45
  20.8 3.7 %collective-permute-start.18 = (s32[8,2,16]{2,1,0:T(2,128)S(1)}, s32[8,2,16]{2,1,0:T(2,128)S(1)}, u32[]{:S(2)}, u32[]{:S(2)}) collective-permute-start(s32[8,2,16]{2,1,0:T(2,128)S(1)} %pad_add_fusion.i0), channel_id=1, source_target_pairs={{0,2},{1,3},{2,0},{3,1},{4,6},{5,7},{6,4},{7,5},{8,10},{9,11},{10,... | collective-permute-start | bytes 3080 | tf_op jit(solution)/shard_map/ppermute | solution.py:45
  24.5 22.9 %collective-permute-start.26 = (bf16[1024,1024]{1,0:T(8,128)(2,1)}, bf16[1024,1024]{1,0:T(8,128)(2,1)S(1)}, u32[]{:S(2)}, u32[]{:S(2)}) collective-permute-start(bf16[1024,1024]{1,0:T(8,128)(2,1)} %refs_9_.3), channel_id=1, source_target_pairs={{0,1},{1,0},{2,3},{3,2},{4,5},{5,4},{6,7},{7,6},{8,9},{9,8},{10,11... | collective-permute-start | bytes 6291464 | tf_op jit(solution)/shard_map/ppermute | solution.py:45
  24.6 22.8 %collective-permute-start.27 = (bf16[1024,1024]{1,0:T(8,128)(2,1)}, bf16[1024,1024]{1,0:T(8,128)(2,1)S(1)}, u32[]{:S(2)}, u32[]{:S(2)}) collective-permute-start(bf16[1024,1024]{1,0:T(8,128)(2,1)} %refs_11_.3), channel_id=1, source_target_pairs={{0,1},{1,0},{2,3},{3,2},{4,5},{5,4},{6,7},{7,6},{8,9},{9,8},{10,11... | collective-permute-start | bytes 6291464 | tf_op jit(solution)/shard_map/ppermute | solution.py:45
  25.0 8.3 %collective-permute-start.21 = (bf16[128,1024]{1,0:T(8,128)(2,1)S(1)}, bf16[128,1024]{1,0:T(8,128)(2,1)S(1)}, u32[]{:S(2)}, u32[]{:S(2)}) collective-permute-start(bf16[128,1024]{1,0:T(8,128)(2,1)S(1)} %half_of.1), channel_id=1, source_target_pairs={{0,2},{1,3},{2,0},{3,1},{4,6},{5,7},{6,4},{7,5},{8,10},{9,11},{10,... | collective-permute-start | bytes 786440 | tf_op jit(solution)/shard_map/ppermute | solution.py:45
  32.6 8.7 %collective-permute-start.20 = (bf16[512,256]{1,0:T(8,128)(2,1)S(1)}, bf16[512,256]{1,0:T(8,128)(2,1)S(1)}, u32[]{:S(2)}, u32[]{:S(2)}) collective-permute-start(bf16[512,256]{1,0:T(8,128)(2,1)S(1)} %get-tuple-element.107.here), channel_id=1, source_target_pairs={{0,2},{1,3},{2,0},{3,1},{4,6},{5,7},{6,4},{7,5},{8,10},{9,11},{10,... | collective-permute-start | bytes 786440 | tf_op jit(solution)/shard_map/ppermute | solution.py:45
  33.3 8.0 %collective-permute-start.22 = (bf16[128,1024]{1,0:T(8,128)(2,1)S(1)}, bf16[128,1024]{1,0:T(8,128)(2,1)S(1)}, u32[]{:S(2)}, u32[]{:S(2)}) collective-permute-start(bf16[128,1024]{1,0:T(8,128)(2,1)S(1)} %collective-permute-done.21.half_0), channel_id=1, source_target_pairs={{0,4},{4,0},{8,12},{12,8},{16,20},{20,16},{24,28},{28,24},{1,5},{5... | collective-permute-start | bytes 786440 | tf_op jit(solution)/shard_map/ppermute | solution.py:45
  39.9 7.5 %collective-permute-start.23 = (bf16[512,256]{1,0:T(8,128)(2,1)S(1)}, bf16[512,256]{1,0:T(8,128)(2,1)S(1)}, u32[]{:S(2)}, u32[]{:S(2)}) collective-permute-start(bf16[512,256]{1,0:T(8,128)(2,1)S(1)} %get-tuple-element.119.context), channel_id=1, source_target_pairs={{0,2},{1,3},{2,0},{3,1},{4,6},{5,7},{6,4},{7,5},{8,10},{9,11},{10,... | collective-permute-start | bytes 786440 | tf_op jit(solution)/shard_map/ppermute | solution.py:45
  41.3 6.0 %collective-permute-start.24 = (bf16[128,1024]{1,0:T(8,128)(2,1)S(1)}, bf16[128,1024]{1,0:T(8,128)(2,1)S(1)}, u32[]{:S(2)}, u32[]{:S(2)}) collective-permute-start(bf16[128,1024]{1,0:T(8,128)(2,1)S(1)} %collective-permute-done.21.half_0), channel_id=1, source_target_pairs={{0,1},{1,0},{2,3},{3,2},{4,5},{5,4},{6,7},{7,6},{8,9},{9,8},{10,11... | collective-permute-start | bytes 786440 | tf_op jit(solution)/shard_map/ppermute | solution.py:45
  41.4 6.0 %collective-permute-start.25 = (bf16[128,1024]{1,0:T(8,128)(2,1)S(1)}, bf16[128,1024]{1,0:T(8,128)(2,1)S(1)}, u32[]{:S(2)}, u32[]{:S(2)}) collective-permute-start(bf16[128,1024]{1,0:T(8,128)(2,1)S(1)} %collective-permute-done.22.half_1), channel_id=1, source_target_pairs={{0,1},{1,0},{2,3},{3,2},{4,5},{5,4},{6,7},{7,6},{8,9},{9,8},{10,11... | collective-permute-start | bytes 786440 | tf_op jit(solution)/shard_map/ppermute | solution.py:45
  51.2 17.3 %collective-permute-start.28 = (bf16[256,1024]{1,0:T(8,128)(2,1)S(1)}, bf16[256,1024]{1,0:T(8,128)(2,1)S(1)}, u32[]{:S(2)}, u32[]{:S(2)}) collective-permute-start(bf16[256,1024]{1,0:T(8,128)(2,1)S(1)} %feed_there.1), channel_id=1, source_target_pairs={{0,2},{1,3},{2,0},{3,1},{4,6},{5,7},{6,4},{7,5},{8,10},{9,11},{10,... | collective-permute-start | bytes 1572872 | tf_op jit(solution)/shard_map/ppermute | solution.py:45
  52.7 8.0 %collective-permute-start.32 = (bf16[1,4,16,1024]{3,2,0,1:T(8,128)(2,1)S(1)}, bf16[1,4,16,1024]{3,2,0,1:T(8,128)(2,1)S(1)}, u32[]{:S(2)}, u32[]{:S(2)}) collective-permute-start(bf16[1,4,16,1024]{3,2,0,1:T(8,128)(2,1)S(1)} %bitcast.71), channel_id=1, source_target_pairs={{0,16},{4,20},{8,24},{12,28},{16,0},{20,4},{24,8},{28,12},{1,17},{... | collective-permute-start | bytes 393224 | tf_op jit(solution)/shard_map/ppermute | solution.py:45
  60.7 4.3 %collective-permute-start.33 = (bf16[2,16,1024]{2,1,0:T(8,128)(2,1)S(1)}, bf16[2,16,1024]{2,1,0:T(8,128)(2,1)S(1)}, u32[]{:S(2)}, u32[]{:S(2)}) collective-permute-start(bf16[2,16,1024]{2,1,0:T(8,128)(2,1)S(1)} %get-tuple-element.172), channel_id=1, source_target_pairs={{0,4},{4,0},{8,12},{12,8},{16,20},{20,16},{24,28},{28,24},{1,5},{5... | collective-permute-start | bytes 196616 | tf_op jit(solution)/shard_map/ppermute | solution.py:45
  62.4 4.3 %collective-permute-start.34 = (bf16[2,16,1024]{2,1,0:T(8,128)(2,1)S(1)}, bf16[2,16,1024]{2,1,0:T(8,128)(2,1)S(1)}, u32[]{:S(2)}, u32[]{:S(2)}) collective-permute-start(bf16[2,16,1024]{2,1,0:T(8,128)(2,1)S(1)} %get-tuple-element.173), channel_id=1, source_target_pairs={{0,8},{4,12},{8,0},{12,4},{16,24},{20,28},{24,16},{28,20},{1,9},{5... | collective-permute-start | bytes 196616 | tf_op jit(solution)/shard_map/ppermute | solution.py:45
  63.1 5.2 %collective-permute-start.35 = (bf16[2,16,1024]{2,1,0:T(8,128)(2,1)S(1)}, bf16[2,16,1024]{2,1,0:T(8,128)(2,1)S(1)}, u32[]{:S(2)}, u32[]{:S(2)}) collective-permute-start(bf16[2,16,1024]{2,1,0:T(8,128)(2,1)S(1)} %get-tuple-element.170), channel_id=1, source_target_pairs={{0,12},{4,8},{8,4},{12,0},{16,28},{20,24},{24,20},{28,16},{1,13},{... | collective-permute-start | bytes 196616 | tf_op jit(solution)/shard_map/ppermute | solution.py:45
  69.7 3.8 %collective-permute-start.38 = (bf16[32,1024]{1,0:T(8,128)(2,1)S(1)}, bf16[32,1024]{1,0:T(8,128)(2,1)S(1)}, u32[]{:S(2)}, u32[]{:S(2)}) collective-permute-start(bf16[32,1024]{1,0:T(8,128)(2,1)S(1)} %get-tuple-element.168), channel_id=1, source_target_pairs={{0,3},{1,2},{2,1},{3,0},{4,7},{5,6},{6,5},{7,4},{8,11},{9,10},{10,... | collective-permute-start | bytes 196616 | tf_op jit(solution)/shard_map/ppermute | solution.py:45
  69.7 5.0 %collective-permute-start.37 = (bf16[32,1024]{1,0:T(8,128)(2,1)S(1)}, bf16[32,1024]{1,0:T(8,128)(2,1)S(1)}, u32[]{:S(2)}, u32[]{:S(2)}) collective-permute-start(bf16[32,1024]{1,0:T(8,128)(2,1)S(1)} %get-tuple-element.169), channel_id=1, source_target_pairs={{0,2},{1,3},{2,0},{3,1},{4,6},{5,7},{6,4},{7,5},{8,10},{9,11},{10,... | collective-permute-start | bytes 196616 | tf_op jit(solution)/shard_map/ppermute | solution.py:45
  70.2 4.6 %collective-permute-start.36 = (bf16[32,1024]{1,0:T(8,128)(2,1)S(1)}, bf16[32,1024]{1,0:T(8,128)(2,1)S(1)}, u32[]{:S(2)}, u32[]{:S(2)}) collective-permute-start(bf16[32,1024]{1,0:T(8,128)(2,1)S(1)} %get-tuple-element.167), channel_id=1, source_target_pairs={{0,1},{1,0},{2,3},{3,2},{4,5},{5,4},{6,7},{7,6},{8,9},{9,8},{10,11... | collective-permute-start | bytes 196616 | tf_op jit(solution)/shard_map/ppermute | solution.py:45
  (18 other events, 90.9 us)
where the time goes:
time: 79.1 us; the launch traced here: 78.8 us
  starting transfers between devices  28.7 us (36%)
  Pallas kernels  27.2 us (34%)
  waiting for transfers between devices  19.2 us (24%)
  other arithmetic  2.09 us (3%)
  between operations  0.9 us (1%)
    ppermute x33, starting transfers between devices, swap(): return lax.ppermute(value, axis, [(i, i ^ mask) for i in range(count)])  28.7 us
    ppermute x33, waiting for transfers between devices, swap(): return lax.ppermute(value, axis, [(i, i ^ mask) for i in range(count)])  19.2 us
    pallas_call x2, Pallas kernels, feed_forward(): pl.pallas_call(lambda *refs: feed_kernel(keep_rest, *refs), out_shape=jax...  7.62 us
    pallas_call x1, Pallas kernels, first_attention(): pl.pallas_call(first_attention_kernel, out_shape=(jax.ShapeDtypeStruct((4...  6.15 us
    pallas_call x1, Pallas kernels, second_attention(): pl.pallas_call(functools.partial(second_attention_kernel, rows_here), out...  4.97 us
    pallas_call x1, Pallas kernels, project_first(): pl.pallas_call(project_first_kernel, out_shape=(jax.ShapeDtypeStruct((seq...  4.12 us
    concatenate x3, other arithmetic, per_device(): held = jnp.concatenate([held, other])  2.05 us
    pallas_call x1, Pallas kernels, score(): pl.pallas_call(score_kernel, out_shape=(jax.ShapeDtypeStruct((2, rows.sha...  1.59 us
  transfers between devices with their start and end apart: 33, of which 16 were waited for; matrix products, arithmetic and copies ran while one was open for 3% of the time, Pallas kernels for 26%

commit v1 on v0

--- a/solution.py
+++ b/solution.py
@@ -57,40 +57,47 @@
     return lax.optimization_barrier((value,) + others)[0]
 
 
-def half_kernel(w_out, half, sem):
+def load_kernel(states, w, w_out, mine, w_here, half, sems):
     part = half.shape[0]
     first = pl.multiple_of((lax.axis_index("req") & 1) * part, part)
-    copy = pltpu.make_async_copy(w_out.at[pl.ds(first, part)], half, sem)
-    copy.start()
-    copy.wait()
-
-
-def half_of(w_out):
-    return pl.pallas_call(
-        half_kernel,
-        out_shape=jax.ShapeDtypeStruct((w_out.shape[0] // 2, w_out.shape[1]), BF16),
-        in_specs=[HBM],
-        out_specs=VMEM,
-        scratch_shapes=[pltpu.SemaphoreType.DMA],
-        compiler_params=params(4),
-        cost_estimate=NO_COST,
-        name="half_of",
-    )(in_hbm(w_out))
-
-
-def first_attention_kernel(
-    lengths, s0, s1, s2, s3, w, b, out, text, own, weights, parts, bias, sems
-):
-    core = lax.axis_index("tp") & 1
-    copies = [pltpu.make_async_copy(s0.at[core], own, sems.at[3])]
-    copies += [pltpu.make_async_copy(w.at[k], weights.at[k], sems.at[k]) for k in range(3)]
+    copies = [
+        pltpu.make_async_copy(source, target, sems.at[number])
+        for number, (source, target) in enumerate(
+            (
+                (w_out.at[pl.ds(first, part)], half),
+                (states.at[lax.axis_index("tp") & 1], mine),
+                (w, w_here),
+            )
+        )
+    ]
     for copy in copies:
         copy.start()
-    copies[0].wait()
-    text[...] = jnp.concatenate([own[...], s1[core], s2[core], s3[core]])
+    for copy in copies:
+        copy.wait()
+
+
+def load(states, w, w_out):
+    return pl.pallas_call(
+        load_kernel,
+        out_shape=(
+            jax.ShapeDtypeStruct(states.shape[1:], BF16),
+            jax.ShapeDtypeStruct(w.shape, BF16),
+            jax.ShapeDtypeStruct((w_out.shape[0] // 2, w_out.shape[1]), BF16),
+        ),
+        in_specs=[HBM] * 3,
+        out_specs=(VMEM, VMEM, VMEM),
+        scratch_shapes=[pltpu.SemaphoreType.DMA((3,))],
+        compiler_params=params(6),
+        cost_estimate=NO_COST,
+        name="load",
+    )(in_hbm(states), in_hbm(w), in_hbm(w_out))
+
+
+def first_attention_kernel(lengths, mine, s1, s2, s3, w, b, out, text, parts, bias):
+    core = lax.axis_index("tp") & 1
+    text[...] = jnp.concatenate([mine[...], s1[core], s2[core], s3[core]])
     for which in range(3):
-        copies[1 + which].wait()
-        project(which, text, weights, b, parts)
+        project(which, text, w, b, parts)
     attend(lengths, parts, bias, out)
 
 
@@ -152,7 +159,7 @@
 
 
 def first_attention(lengths, blocks, w, b):
-    _, share, width = blocks[0].shape
+    share, width = blocks[0].shape
     wide = w.shape[2]
     return pl.pallas_call(
         first_attention_kernel,
@@ -160,27 +167,25 @@
             jax.ShapeDtypeStruct((4 * share, wide), BF16),
             jax.ShapeDtypeStruct((4 * share, width), BF16),
         ),
-        in_specs=[SMEM, HBM] + [VMEM] * 3 + [HBM, VMEM],
+        in_specs=[SMEM] + [VMEM] * 6,
         out_specs=(VMEM, VMEM),
-        scratch_shapes=[pltpu.VMEM((share, width), BF16), pltpu.VMEM(w.shape, BF16)]
-        + attention_scratch(4 * share, wide)
-        + [pltpu.SemaphoreType.DMA((4,))],
-        compiler_params=params(14),
+        scratch_shapes=attention_scratch(4 * share, wide),
+        compiler_params=params(12),
         cost_estimate=NO_COST,
         name="attention_own",
-    )(in_hbm(lengths), in_hbm(blocks[0]), *blocks[1:], in_hbm(w), in_hbm(b))
+    )(in_hbm(lengths), *blocks, w, in_hbm(b))
 
 
 def second_attention(lengths, text, w, b, ids, rows_here):
     seq_len = text.shape[0]
     wide = w.shape[2]
-    groups, _, each = ids[0].shape
+    groups, each = ids[0].shape
     return pl.pallas_call(
         functools.partial(second_attention_kernel, rows_here),
         out_shape=(
             jax.ShapeDtypeStruct((seq_len, wide), BF16),
             jax.ShapeDtypeStruct((2, groups * SLOTS), I32),
-            jax.ShapeDtypeStruct((groups * SLOTS, 8 * each), BF16),
+            jax.ShapeDtypeStruct((groups * SLOTS, 4 * each), BF16),
             jax.ShapeDtypeStruct((1,), I32),
         ),
         in_specs=[SMEM] + [VMEM] * 7,
@@ -390,7 +395,7 @@
     group = lax.axis_index("req")
     groups = parts[0].shape[0]
     slots = groups * SLOTS
-    ids = jnp.concatenate([part[:, text, :] for part in parts for text in range(2)], axis=1)
+    ids = jnp.concatenate([part[...] for part in parts], axis=1)
     count = ids.shape[1]
     owner = lax.shift_right_logical(ids, I32(rows_here.bit_length() - 1))
     before = as_ones(
@@ -504,7 +509,7 @@
 
 
 def take_rows(number, ids, index_rows):
-    groups, _, each = ids[0].shape
+    groups, each = ids[0].shape
     slots = groups * SLOTS
     width = index_rows.shape[1]
     half = jax.ShapeDtypeStruct((slots // 2, width), BF16)
@@ -513,7 +518,7 @@
         out_shape=(
             half,
             half,
-            jax.ShapeDtypeStruct((slots, 8 * each), BF16),
+            jax.ShapeDtypeStruct((slots, 4 * each), BF16),
             jax.ShapeDtypeStruct((1,), I32),
         ),
         in_specs=[SMEM] + [VMEM] * 4 + [HBM],
@@ -609,26 +614,26 @@
     b_qkv_p = swap(b_qkv, "tp", 1)
     b_up_p = swap(b_up, "tp", 1)
 
-    held = cand_ids[None]
+    held = cand_ids.reshape(1, -1)
     for mask in masks("req"):
         other = swap(held, "req", mask)
         if mask * 2 == lax.axis_size("req"):
-            w_half = half_of(after(w_out, held))
-            other, w_half = lax.optimization_barrier((other, w_half))
+            mine, w_here, w_half = load(states, w_qkv_t, after(w_out, held))
+            other, mine = lax.optimization_barrier((other, mine))
         held = jnp.concatenate([held, other])
-    w_out_p = swap(w_out, "tp", 1)
-    from_chip, held, from_core, w_qkv_p, b_qkv_p, b_up_p, w_out_p = lax.optimization_barrier(
-        (from_chip, held, from_core, w_qkv_p, b_qkv_p, b_up_p, w_out_p)
-    )
+    from_chip, held, from_core, w_qkv_p, b_qkv_p, b_up_p = lax.optimization_barrier(
+        (from_chip, held, from_core, w_qkv_p, b_qkv_p, b_up_p)
+    )
+    w_out_p = swap(after(w_out, from_chip), "tp", 1)
     from_diag = swap(from_chip, "tp", 1)
-    blocks = (states, from_core, from_chip, from_diag)
+    blocks = (mine, from_core, from_chip, from_diag)
     ids = (held,) + tuple(swap(held, "tp", mask) for mask in (1, 2, 3))
-    w_up_p = swap(after(w_up, from_diag, *ids), "tp", 1)
-    w_down_p = swap(after(w_down, from_diag, *ids), "tp", 1)
+    w_up_p = swap(after(w_up, from_diag, w_out_p, *ids), "tp", 1)
+    w_down_p = swap(after(w_down, from_diag, w_out_p, *ids), "tp", 1)
     w_x0 = swap(after(w_half, ids[2]), "tp", 2)
 
-    blocks, ids = lax.optimization_barrier((blocks, ids))
-    context_0, text = first_attention(lengths, blocks, w_qkv_t, b_qkv)
+    blocks, ids, w_out_p = lax.optimization_barrier((blocks, ids, w_out_p))
+    context_0, text = first_attention(lengths, blocks, w_here, b_qkv)
     context_0x = swap(context_0, "tp", 2)
     w_x1 = swap(after(w_x0, context_0), "req", 1)
     context_1, numbers, place, rounds = second_attention(
@@ -657,7 +662,7 @@
         lengths, down_here, down_x, ln2_gain[None], ln2_shift[None]
     )
 
-    rows = gathered(keep, after(send, down_there), (down_here,), (down_here,), (hidden,))
+    rows = gathered(keep, send, (down_there,), (down_here,), ())
     pools = (pool,) + tuple(swap(pool, "tp", mask) for mask in (1, 2, 3))
     hidden_p = swap(hidden_other, "tp", 1)
     rows = further(after(rows, *pools))

time: 79.1 us -> 77.2 us (0.976)
  waiting for transfers between devices: 19.2 us -> 12.4 us
  Pallas kernels: 27.2 us -> 31 us
  local copies, waits for them, and re-layouts: 0.06 us -> 2.99 us
  other arithmetic: 2.09 us -> 0.07 us
    ppermute x33, waiting for transfers between devices: 19.2 us -> 12.4 us  [swap(): return lax.ppermute(value, axis, [(i, i ^ mask) for i in range(count)])]
    pallas_call x2, Pallas kernels: 7.62 us -> 12.8 us  [feed_forward(): pl.pallas_call(lambda *refs: feed_kernel(keep_rest, *refs), out_shape=jax...]
    unnamed x18 -> x28, local copies, waits for them, and re-layouts: 0.04 us -> 2.22 us
    concatenate x3, other arithmetic: 2.05 us -> 0.03 us  [per_device(): held = jnp.concatenate([held, other])]
    pallas_call x1, Pallas kernels: 6.15 us -> 4.2 us  [first_attention(): pl.pallas_call(first_attention_kernel, out_shape=(jax.ShapeDtypeStruct((4...]
  transfers between devices with their start and end apart: 33 -> 33, of which waited for: 16 -> 13; matrix products, arithmetic and copies ran while one was open for 3% -> 1% of each run, Pallas kernels for 26% -> 38%
where the time goes in v1:
time: 77.2 us
  Pallas kernels  31 us (40%)
  starting transfers between devices  29.2 us (38%)
  waiting for transfers between devices  12.4 us (16%)
  local copies, waits for them, and re-layouts  2.99 us (4%)
  between operations  0.96 us (1%)
    ppermute x33, starting transfers between devices, swap(): return lax.ppermute(value, axis, [(i, i ^ mask) for i in range(count)])  29.2 us
    pallas_call x2, Pallas kernels, feed_forward(): pl.pallas_call(lambda *refs: feed_kernel(keep_rest, *refs), out_shape=jax...  12.8 us
    ppermute x33, waiting for transfers between devices, swap(): return lax.ppermute(value, axis, [(i, i ^ mask) for i in range(count)])  12.4 us
    pallas_call x1, Pallas kernels, second_attention(): pl.pallas_call(functools.partial(second_attention_kernel, rows_here), out...  4.96 us
    pallas_call x1, Pallas kernels, first_attention(): pl.pallas_call(first_attention_kernel, out_shape=(jax.ShapeDtypeStruct((4...  4.2 us
    pallas_call x1, Pallas kernels, project_first(): pl.pallas_call(project_first_kernel, out_shape=(jax.ShapeDtypeStruct((seq...  4 us
    unnamed x28, local copies, waits for them, and re-layouts  2.22 us
    pallas_call x1, Pallas kernels, load(): pl.pallas_call(load_kernel, out_shape=(jax.ShapeDtypeStruct(states.shape[...  1.61 us
  transfers between devices with their start and end apart: 33, of which 13 were waited for; matrix products, arithmetic and copies ran while one was open for 1% of the time, Pallas kernels for 38%

profile of v1, /device:TPU:0, one launch (start us, length us, event | category | flops | bytes accessed | tf_op | source)
XLA Modules:
  0.0 77.2 jit_solution(1535026731173994524)
XLA Ops:
  1.2 2.6 %collective-permute-start.10 = (bf16[2,128,1024]{2,1,0:T(8,128)(2,1)}, bf16[2,128,1024]{2,1,0:T(8,128)(2,1)S(1)}, u32[]{:S(2)}, u32[]{:S(2)}) collective-permute-start(bf16[2,128,1024]{2,1,0:T(8,128)(2,1)} %states.1), channel_id=1, source_target_pairs={{0,2},{1,3},{2,0},{3,1},{4,6},{5,7},{6,4},{7,5},{8,10},{9,11},{10,... | collective-permute-start | bytes 1572872 | tf_op jit(solution)/shard_map/ppermute | solution.py:45
  4.7 1.5 %collective-permute-start.7 = (s32[1,32]{1,0:T(1,128)S(1)}, s32[1,32]{1,0:T(1,128)S(1)}, u32[]{:S(2)}, u32[]{:S(2)}) collective-permute-start(s32[1,32]{1,0:T(1,128)S(1)} %reshape.58), channel_id=1, source_target_pairs={{0,4},{4,0},{8,12},{12,8},{16,20},{20,16},{24,28},{28,24},{1,5},{5... | collective-permute-start | bytes 392 | tf_op jit(solution)/shard_map/ppermute | solution.py:45
  6.2 2.0 %collective-permute-done.7 = s32[1,32]{1,0:T(1,128)S(1)} collective-permute-done((s32[1,32]{1,0:T(1,128)S(1)}, s32[1,32]{1,0:T(1,128)S(1)}, u32[]{:S(2)}, u32[]{:S(2)}) %collective-permute-start.7) | collective-permute-done | bytes 160 | tf_op jit(solution)/shard_map/ppermute | solution.py:45
  8.2 1.6 %collective-permute-start.8 = (s32[2,32]{1,0:T(2,128)S(1)}, s32[2,32]{1,0:T(2,128)S(1)}, u32[]{:S(2)}, u32[]{:S(2)}) collective-permute-start(s32[2,32]{1,0:T(2,128)S(1)} %pad_add_fusion.2), channel_id=1, source_target_pairs={{0,8},{4,12},{8,0},{12,4},{16,24},{20,28},{24,16},{28,20},{1,9},{5... | collective-permute-start | bytes 776 | tf_op jit(solution)/shard_map/ppermute | solution.py:45
  9.9 2.0 %collective-permute-done.8 = s32[2,32]{1,0:T(2,128)S(1)} collective-permute-done((s32[2,32]{1,0:T(2,128)S(1)}, s32[2,32]{1,0:T(2,128)S(1)}, u32[]{:S(2)}, u32[]{:S(2)}) %collective-permute-start.8) | collective-permute-done | bytes 288 | tf_op jit(solution)/shard_map/ppermute | solution.py:45
  11.9 2.7 %collective-permute-start.9 = (s32[4,32]{1,0:T(4,128)S(1)}, s32[4,32]{1,0:T(4,128)S(1)}, u32[]{:S(2)}, u32[]{:S(2)}) collective-permute-start(s32[4,32]{1,0:T(4,128)S(1)} %pad_add_fusion.1), channel_id=1, source_target_pairs={{0,16},{4,20},{8,24},{12,28},{16,0},{20,4},{24,8},{28,12},{1,17},{... | collective-permute-start | bytes 1544 | tf_op jit(solution)/shard_map/ppermute | solution.py:45
  14.5 1.6 %load.1 = (bf16[128,1024]{1,0:T(8,128)(2,1)S(1)}, bf16[3,1024,256]{2,1,0:T(8,128)(2,1)S(1)}, bf16[128,1024]{1,0:T(8,128)(2,1)S(1)}) custom-call(bf16[2,128,1024]{2,1,0:T(8,128)(2,1)} %states.1, bf16[3,1024,256]{2,1,0:T(8,128)(2,1)} %bitcast.85, bf16[256,1024]{1,0:T(8,128)(2,1)} %w.1), custom_call_target="tpu_custom_call" | custom-call | flops 1 | bytes 1 | tf_op jit(solution)/shard_map/load/pallas_call | solution.py:80
  17.6 1.2 %copy-done.5 = bf16[3,1024,256]{2,1,0:T(8,128)(2,1)} copy-done((bf16[3,1024,256]{2,1,0:T(8,128)(2,1)}, bf16[3,1024,256]{2,1,0:T(8,128)(2,1)S(1)}, u32[]{:S(2)}) %copy-start.5) | copy-done | bytes 1572888
  21.5 1.8 %collective-permute-done.17.i2 = s32[8,32]{1,0:T(8,128)S(1)} collective-permute-done((s32[8,32]{1,0:T(8,128)S(1)}, s32[8,32]{1,0:T(8,128)S(1)}, u32[]{:S(2)}, u32[]{:S(2)}) %collective-permute-start.17) | collective-permute-done | bytes 1056 | tf_op jit(solution)/shard_map/ppermute | solution.py:45
  23.8 1.4 %collective-permute-start.21 = (bf16[128,1024]{1,0:T(8,128)(2,1)S(1)}, bf16[128,1024]{1,0:T(8,128)(2,1)S(1)}, u32[]{:S(2)}, u32[]{:S(2)}) collective-permute-start(bf16[128,1024]{1,0:T(8,128)(2,1)S(1)} %get-tuple-element.115), channel_id=1, source_target_pairs={{0,2},{1,3},{2,0},{3,1},{4,6},{5,7},{6,4},{7,5},{8,10},{9,11},{10,... | collective-permute-start | bytes 786440 | tf_op jit(solution)/shard_map/ppermute | solution.py:45
  25.2 4.2 %attention_own.1 = (bf16[512,256]{1,0:T(8,128)(2,1)S(1)}, bf16[512,1024]{1,0:T(8,128)(2,1)S(1)}) custom-call(s32[2]{0:T(128)} %lengths.7, bf16[128,1024]{1,0:T(8,128)(2,1)S(1)} %get-tuple-element.107.mine, bf16[2,128,1024]{2,1,0:T(8,128)(2,1)S(1)} %collective-permute-done.11.s1, bf16[2,128,1024]{2,1,0:T(8,128)(2,1)S(1)} %collective-permute-done.10.s2, ...), custom_call_target="tpu_custom_call" | custom-call | flops 1 | bytes 1 | tf_op jit(solution)/shard_map/attention_own/pallas_call | solution.py:164
  30.2 2.1 %collective-permute-done.21.half_0 = bf16[128,1024]{1,0:T(8,128)(2,1)S(1)} collective-permute-done((bf16[128,1024]{1,0:T(8,128)(2,1)S(1)}, bf16[128,1024]{1,0:T(8,128)(2,1)S(1)}, u32[]{:S(2)}, u32[]{:S(2)}) %collective-permute-start.21) | collective-permute-done | bytes 262176 | tf_op jit(solution)/shard_map/ppermute | solution.py:45
  32.3 1.5 %collective-permute-start.22 = (bf16[128,1024]{1,0:T(8,128)(2,1)S(1)}, bf16[128,1024]{1,0:T(8,128)(2,1)S(1)}, u32[]{:S(2)}, u32[]{:S(2)}) collective-permute-start(bf16[128,1024]{1,0:T(8,128)(2,1)S(1)} %collective-permute-done.21.half_0), channel_id=1, source_target_pairs={{0,4},{4,0},{8,12},{12,8},{16,20},{20,16},{24,28},{28,24},{1,5},{5... | collective-permute-start | bytes 786440 | tf_op jit(solution)/shard_map/ppermute | solution.py:45
  33.8 5.0 %attention_partner.1 = (bf16[512,256]{1,0:T(8,128)(2,1)S(1)}, s32[2,128]{1,0:T(2,128)S(1)}, bf16[128,128]{1,0:T(8,128)(2,1)S(1)}, s32[1]{0:T(128)}) custom-call(s32[2]{0:T(128)} %lengths.7, bf16[512,1024]{1,0:T(8,128)(2,1)S(1)} %get-tuple-element.112.text, bf16[3,1024,256]{2,1,0:T(8,128)(2,1)S(1)} %copy-done.6, f32[3,256]{1,0:T(4,128)S(1)} %collective-permute-done.13.b, ...), custom_call_target="tpu_custom_call" | custom-call | flops 6000000000 | bytes 1048576 | tf_op jit(solution)/shard_map/attention_partner/pallas_call | solution.py:183
  38.8 2.2 %collective-permute-start.23 = (bf16[512,256]{1,0:T(8,128)(2,1)S(1)}, bf16[512,256]{1,0:T(8,128)(2,1)}, u32[]{:S(2)}, u32[]{:S(2)}) collective-permute-start(bf16[512,256]{1,0:T(8,128)(2,1)S(1)} %get-tuple-element.125.context), channel_id=1, source_target_pairs={{0,2},{1,3},{2,0},{3,1},{4,6},{5,7},{6,4},{7,5},{8,10},{9,11},{10,... | collective-permute-start | bytes 786440 | tf_op jit(solution)/shard_map/ppermute | solution.py:45
  42.4 4.0 %project_first.1 = (f32[512,1024]{1,0:T(8,128)S(1)}, bf16[64,1024]{1,0:T(8,128)(2,1)S(1)}, bf16[64,1024]{1,0:T(8,128)(2,1)S(1)}) custom-call(bf16[512,1024]{1,0:T(8,128)(2,1)S(1)} %get-tuple-element.112.text, bf16[512,256]{1,0:T(8,128)(2,1)S(1)} %copy-done.2, bf16[512,256]{1,0:T(8,128)(2,1)S(1)} %collective-permute-done.20.there, ...), custom_call_target="tpu_custom_call" | custom-call | flops 1000000000 | bytes 1048576 | tf_op jit(solution)/shard_map/project_first/pallas_call | solution.py:229
  47.0 2.9 %collective-permute-start.32 = (bf16[1,4,16,1024]{3,2,0,1:T(8,128)(2,1)S(1)}, bf16[1,4,16,1024]{3,2,0,1:T(8,128)(2,1)S(1)}, u32[]{:S(2)}, u32[]{:S(2)}) collective-permute-start(bf16[1,4,16,1024]{3,2,0,1:T(8,128)(2,1)S(1)} %bitcast.70), channel_id=1, source_target_pairs={{0,16},{4,20},{8,24},{12,28},{16,0},{20,4},{24,8},{28,12},{1,17},{... | collective-permute-start | bytes 393224 | tf_op jit(solution)/shard_map/ppermute | solution.py:45
  49.9 6.2 %feed_there.1 = bf16[256,1024]{1,0:T(8,128)(2,1)S(1)} custom-call(f32[512,1024]{1,0:T(8,128)S(1)} %project_second.1.refs_0_, bf16[512,256]{1,0:T(8,128)(2,1)} %collective-permute-done.23.refs_1_, bf16[128,1024]{1,0:T(8,128)(2,1)} %collective-permute-done.24.refs_2_, bf16[128,1024]{1,0:T(8,128)(2,1)} %collective-permute-done.25.refs_3_, ...), custom_call_target="tpu_custom_call" | custom-call | flops 8000000000 | bytes 1048576 | tf_op jit(solution)/shard_map/feed_there/pallas_call | solution.py:294
  57.6 1.5 %collective-permute-start.34 = (bf16[2,16,1024]{2,1,0:T(8,128)(2,1)S(1)}, bf16[2,16,1024]{2,1,0:T(8,128)(2,1)S(1)}, u32[]{:S(2)}, u32[]{:S(2)}) collective-permute-start(bf16[2,16,1024]{2,1,0:T(8,128)(2,1)S(1)} %get-tuple-element.177), channel_id=1, source_target_pairs={{0,8},{4,12},{8,0},{12,4},{16,24},{20,28},{24,16},{28,20},{1,9},{5... | collective-permute-start | bytes 196616 | tf_op jit(solution)/shard_map/ppermute | solution.py:45
  59.0 1.3 %collective-permute-start.35 = (bf16[2,16,1024]{2,1,0:T(8,128)(2,1)S(1)}, bf16[2,16,1024]{2,1,0:T(8,128)(2,1)S(1)}, u32[]{:S(2)}, u32[]{:S(2)}) collective-permute-start(bf16[2,16,1024]{2,1,0:T(8,128)(2,1)S(1)} %get-tuple-element.174), channel_id=1, source_target_pairs={{0,12},{4,8},{8,4},{12,0},{16,28},{20,24},{24,20},{28,16},{1,13},{... | collective-permute-start | bytes 196616 | tf_op jit(solution)/shard_map/ppermute | solution.py:45
  60.3 6.6 %feed_here.1.here = f32[256,1024]{1,0:T(8,128)S(1)} custom-call(f32[512,1024]{1,0:T(8,128)S(1)} %project_second.1.refs_0_, bf16[512,256]{1,0:T(8,128)(2,1)} %collective-permute-done.23.refs_1_, bf16[128,1024]{1,0:T(8,128)(2,1)} %collective-permute-done.24.refs_2_, bf16[128,1024]{1,0:T(8,128)(2,1)} %collective-permute-done.25.refs_3_, ...), custom_call_target="tpu_custom_call" | custom-call | flops 8000000000 | bytes 1048576 | tf_op jit(solution)/shard_map/feed_here/pallas_call | solution.py:294
  67.3 1.6 %collective-permute-start.37 = (bf16[32,1024]{1,0:T(8,128)(2,1)S(1)}, bf16[32,1024]{1,0:T(8,128)(2,1)S(1)}, u32[]{:S(2)}, u32[]{:S(2)}) collective-permute-start(bf16[32,1024]{1,0:T(8,128)(2,1)S(1)} %get-tuple-element.173), channel_id=1, source_target_pairs={{0,2},{1,3},{2,0},{3,1},{4,6},{5,7},{6,4},{7,5},{8,10},{9,11},{10,... | collective-permute-start | bytes 196616 | tf_op jit(solution)/shard_map/ppermute | solution.py:45
  73.2 1.3 %collective-permute-done.30.pool_chip = f32[1,1024]{1,0:T(1,128)S(1)} collective-permute-done((f32[1,1024]{1,0:T(1,128)S(1)}, f32[1,1024]{1,0:T(1,128)S(1)}, u32[]{:S(2)}, u32[]{:S(2)}) %collective-permute-start.30) | collective-permute-done | bytes 4128 | tf_op jit(solution)/shard_map/ppermute | solution.py:45
  75.6 1.6 %score.1 = (f32[2,16]{1,0:T(2,128)}, bf16[2,128,1024]{2,1,0:T(8,128)(2,1)}) custom-call(s32[2]{0:T(128)S(1)} %copy-done.4, f32[1,1024]{1,0:T(1,128)S(1)} %get-tuple-element.133.pool, f32[1,1024]{1,0:T(1,128)S(1)} %collective-permute-done.29.pool_core, f32[1,1024]{1,0:T(1,128)S(1)} %collective-permute-done.30.pool_chip, ...), custom_call_target="tpu_custom_call" | custom-call | flops 1000000000 | bytes 1048576 | tf_op jit(solution)/shard_map/score/pallas_call | solution.py:366
  (88 shorter events, 16.0 us)
Async XLA Ops:
  0.7 16.9 %collective-permute-start.12 = (bf16[3,1024,256]{2,1,0:T(8,128)(2,1)}, bf16[3,1024,256]{2,1,0:T(8,128)(2,1)S(1)}, u32[]{:S(2)}, u32[]{:S(2)}) collective-permute-start(bf16[3,1024,256]{2,1,0:T(8,128)(2,1)} %bitcast.84), channel_id=1, source_target_pairs={{0,1},{1,0},{2,3},{3,2},{4,5},{5,4},{6,7},{7,6},{8,9},{9,8},{10,11... | collective-permute-start | bytes 4718600 | tf_op jit(solution)/shard_map/ppermute | solution.py:45
  1.2 16.4 %collective-permute-start.10 = (bf16[2,128,1024]{2,1,0:T(8,128)(2,1)}, bf16[2,128,1024]{2,1,0:T(8,128)(2,1)S(1)}, u32[]{:S(2)}, u32[]{:S(2)}) collective-permute-start(bf16[2,128,1024]{2,1,0:T(8,128)(2,1)} %states.1), channel_id=1, source_target_pairs={{0,2},{1,3},{2,0},{3,1},{4,6},{5,7},{6,4},{7,5},{8,10},{9,11},{10,... | collective-permute-start | bytes 1572872 | tf_op jit(solution)/shard_map/ppermute | solution.py:45
  3.7 13.8 %collective-permute-start.11 = (bf16[2,128,1024]{2,1,0:T(8,128)(2,1)}, bf16[2,128,1024]{2,1,0:T(8,128)(2,1)S(1)}, u32[]{:S(2)}, u32[]{:S(2)}) collective-permute-start(bf16[2,128,1024]{2,1,0:T(8,128)(2,1)} %states.1), channel_id=1, source_target_pairs={{0,1},{1,0},{2,3},{3,2},{4,5},{5,4},{6,7},{7,6},{8,9},{9,8},{10,11... | collective-permute-start | bytes 1572872 | tf_op jit(solution)/shard_map/ppermute | solution.py:45
  8.2 3.6 %collective-permute-start.8 = (s32[2,32]{1,0:T(2,128)S(1)}, s32[2,32]{1,0:T(2,128)S(1)}, u32[]{:S(2)}, u32[]{:S(2)}) collective-permute-start(s32[2,32]{1,0:T(2,128)S(1)} %pad_add_fusion.2), channel_id=1, source_target_pairs={{0,8},{4,12},{8,0},{12,4},{16,24},{20,28},{24,16},{28,20},{1,9},{5... | collective-permute-start | bytes 776 | tf_op jit(solution)/shard_map/ppermute | solution.py:45
  11.9 4.5 %collective-permute-start.9 = (s32[4,32]{1,0:T(4,128)S(1)}, s32[4,32]{1,0:T(4,128)S(1)}, u32[]{:S(2)}, u32[]{:S(2)}) collective-permute-start(s32[4,32]{1,0:T(4,128)S(1)} %pad_add_fusion.1), channel_id=1, source_target_pairs={{0,16},{4,20},{8,24},{12,28},{16,0},{20,4},{24,8},{28,12},{1,17},{... | collective-permute-start | bytes 1544 | tf_op jit(solution)/shard_map/ppermute | solution.py:45
  18.8 4.4 %collective-permute-start.15 = (bf16[2,128,1024]{2,1,0:T(8,128)(2,1)S(1)}, bf16[2,128,1024]{2,1,0:T(8,128)(2,1)S(1)}, u32[]{:S(2)}, u32[]{:S(2)}) collective-permute-start(bf16[2,128,1024]{2,1,0:T(8,128)(2,1)S(1)} %collective-permute-done.10.s2), channel_id=1, source_target_pairs={{0,1},{1,0},{2,3},{3,2},{4,5},{5,4},{6,7},{7,6},{8,9},{9,8},{10,11... | collective-permute-start | bytes 1572872 | tf_op jit(solution)/shard_map/ppermute | solution.py:45
  19.1 4.1 %collective-permute-start.19 = (bf16[256,1024]{1,0:T(8,128)(2,1)S(1)}, bf16[256,1024]{1,0:T(8,128)(2,1)S(1)}, u32[]{:S(2)}, u32[]{:S(2)}) collective-permute-start(bf16[256,1024]{1,0:T(8,128)(2,1)S(1)} %copy-done), channel_id=1, source_target_pairs={{0,1},{1,0},{2,3},{3,2},{4,5},{5,4},{6,7},{7,6},{8,9},{9,8},{10,11... | collective-permute-start | bytes 1572872 | tf_op jit(solution)/shard_map/ppermute | solution.py:45
  23.3 26.6 %collective-permute-start.26 = (bf16[1024,1024]{1,0:T(8,128)(2,1)}, bf16[1024,1024]{1,0:T(8,128)(2,1)}, u32[]{:S(2)}, u32[]{:S(2)}) collective-permute-start(bf16[1024,1024]{1,0:T(8,128)(2,1)} %refs_9_.3), channel_id=1, source_target_pairs={{0,1},{1,0},{2,3},{3,2},{4,5},{5,4},{6,7},{7,6},{8,9},{9,8},{10,11... | collective-permute-start | bytes 6291464 | tf_op jit(solution)/shard_map/ppermute | solution.py:45
  23.4 26.5 %collective-permute-start.27 = (bf16[1024,1024]{1,0:T(8,128)(2,1)}, bf16[1024,1024]{1,0:T(8,128)(2,1)}, u32[]{:S(2)}, u32[]{:S(2)}) collective-permute-start(bf16[1024,1024]{1,0:T(8,128)(2,1)} %refs_11_.3), channel_id=1, source_target_pairs={{0,1},{1,0},{2,3},{3,2},{4,5},{5,4},{6,7},{7,6},{8,9},{9,8},{10,11... | collective-permute-start | bytes 6291464 | tf_op jit(solution)/shard_map/ppermute | solution.py:45
  23.8 8.4 %collective-permute-start.21 = (bf16[128,1024]{1,0:T(8,128)(2,1)S(1)}, bf16[128,1024]{1,0:T(8,128)(2,1)S(1)}, u32[]{:S(2)}, u32[]{:S(2)}) collective-permute-start(bf16[128,1024]{1,0:T(8,128)(2,1)S(1)} %get-tuple-element.115), channel_id=1, source_target_pairs={{0,2},{1,3},{2,0},{3,1},{4,6},{5,7},{6,4},{7,5},{8,10},{9,11},{10,... | collective-permute-start | bytes 786440 | tf_op jit(solution)/shard_map/ppermute | solution.py:45
  29.4 11.5 %collective-permute-start.20 = (bf16[512,256]{1,0:T(8,128)(2,1)S(1)}, bf16[512,256]{1,0:T(8,128)(2,1)S(1)}, u32[]{:S(2)}, u32[]{:S(2)}) collective-permute-start(bf16[512,256]{1,0:T(8,128)(2,1)S(1)} %get-tuple-element.113.here), channel_id=1, source_target_pairs={{0,2},{1,3},{2,0},{3,1},{4,6},{5,7},{6,4},{7,5},{8,10},{9,11},{10,... | collective-permute-start | bytes 786440 | tf_op jit(solution)/shard_map/ppermute | solution.py:45
  32.3 8.7 %collective-permute-start.22 = (bf16[128,1024]{1,0:T(8,128)(2,1)S(1)}, bf16[128,1024]{1,0:T(8,128)(2,1)S(1)}, u32[]{:S(2)}, u32[]{:S(2)}) collective-permute-start(bf16[128,1024]{1,0:T(8,128)(2,1)S(1)} %collective-permute-done.21.half_0), channel_id=1, source_target_pairs={{0,4},{4,0},{8,12},{12,8},{16,20},{20,16},{24,28},{28,24},{1,5},{5... | collective-permute-start | bytes 786440 | tf_op jit(solution)/shard_map/ppermute | solution.py:45
  38.8 8.2 %collective-permute-start.23 = (bf16[512,256]{1,0:T(8,128)(2,1)S(1)}, bf16[512,256]{1,0:T(8,128)(2,1)}, u32[]{:S(2)}, u32[]{:S(2)}) collective-permute-start(bf16[512,256]{1,0:T(8,128)(2,1)S(1)} %get-tuple-element.125.context), channel_id=1, source_target_pairs={{0,2},{1,3},{2,0},{3,1},{4,6},{5,7},{6,4},{7,5},{8,10},{9,11},{10,... | collective-permute-start | bytes 786440 | tf_op jit(solution)/shard_map/ppermute | solution.py:45
  40.9 8.9 %collective-permute-start.24 = (bf16[128,1024]{1,0:T(8,128)(2,1)S(1)}, bf16[128,1024]{1,0:T(8,128)(2,1)}, u32[]{:S(2)}, u32[]{:S(2)}) collective-permute-start(bf16[128,1024]{1,0:T(8,128)(2,1)S(1)} %collective-permute-done.21.half_0), channel_id=1, source_target_pairs={{0,1},{1,0},{2,3},{3,2},{4,5},{5,4},{6,7},{7,6},{8,9},{9,8},{10,11... | collective-permute-start | bytes 786440 | tf_op jit(solution)/shard_map/ppermute | solution.py:45
  41.0 8.9 %collective-permute-start.25 = (bf16[128,1024]{1,0:T(8,128)(2,1)S(1)}, bf16[128,1024]{1,0:T(8,128)(2,1)}, u32[]{:S(2)}, u32[]{:S(2)}) collective-permute-start(bf16[128,1024]{1,0:T(8,128)(2,1)S(1)} %collective-permute-done.22.half_1), channel_id=1, source_target_pairs={{0,1},{1,0},{2,3},{3,2},{4,5},{5,4},{6,7},{7,6},{8,9},{9,8},{10,11... | collective-permute-start | bytes 786440 | tf_op jit(solution)/shard_map/ppermute | solution.py:45
  47.0 9.7 %collective-permute-start.32 = (bf16[1,4,16,1024]{3,2,0,1:T(8,128)(2,1)S(1)}, bf16[1,4,16,1024]{3,2,0,1:T(8,128)(2,1)S(1)}, u32[]{:S(2)}, u32[]{:S(2)}) collective-permute-start(bf16[1,4,16,1024]{3,2,0,1:T(8,128)(2,1)S(1)} %bitcast.70), channel_id=1, source_target_pairs={{0,16},{4,20},{8,24},{12,28},{16,0},{20,4},{24,8},{28,12},{1,17},{... | collective-permute-start | bytes 393224 | tf_op jit(solution)/shard_map/ppermute | solution.py:45
  56.2 13.4 %collective-permute-start.28 = (bf16[256,1024]{1,0:T(8,128)(2,1)S(1)}, bf16[256,1024]{1,0:T(8,128)(2,1)S(1)}, u32[]{:S(2)}, u32[]{:S(2)}) collective-permute-start(bf16[256,1024]{1,0:T(8,128)(2,1)S(1)} %feed_there.1), channel_id=1, source_target_pairs={{0,2},{1,3},{2,0},{3,1},{4,6},{5,7},{6,4},{7,5},{8,10},{9,11},{10,... | collective-permute-start | bytes 1572872 | tf_op jit(solution)/shard_map/ppermute | solution.py:45
  56.7 10.1 %collective-permute-start.33 = (bf16[2,16,1024]{2,1,0:T(8,128)(2,1)S(1)}, bf16[2,16,1024]{2,1,0:T(8,128)(2,1)S(1)}, u32[]{:S(2)}, u32[]{:S(2)}) collective-permute-start(bf16[2,16,1024]{2,1,0:T(8,128)(2,1)S(1)} %get-tuple-element.176), channel_id=1, source_target_pairs={{0,4},{4,0},{8,12},{12,8},{16,20},{20,16},{24,28},{28,24},{1,5},{5... | collective-permute-start | bytes 196616 | tf_op jit(solution)/shard_map/ppermute | solution.py:45
  57.6 9.3 %collective-permute-start.34 = (bf16[2,16,1024]{2,1,0:T(8,128)(2,1)S(1)}, bf16[2,16,1024]{2,1,0:T(8,128)(2,1)S(1)}, u32[]{:S(2)}, u32[]{:S(2)}) collective-permute-start(bf16[2,16,1024]{2,1,0:T(8,128)(2,1)S(1)} %get-tuple-element.177), channel_id=1, source_target_pairs={{0,8},{4,12},{8,0},{12,4},{16,24},{20,28},{24,16},{28,20},{1,9},{5... | collective-permute-start | bytes 196616 | tf_op jit(solution)/shard_map/ppermute | solution.py:45
  59.0 7.9 %collective-permute-start.35 = (bf16[2,16,1024]{2,1,0:T(8,128)(2,1)S(1)}, bf16[2,16,1024]{2,1,0:T(8,128)(2,1)S(1)}, u32[]{:S(2)}, u32[]{:S(2)}) collective-permute-start(bf16[2,16,1024]{2,1,0:T(8,128)(2,1)S(1)} %get-tuple-element.174), channel_id=1, source_target_pairs={{0,12},{4,8},{8,4},{12,0},{16,28},{20,24},{24,20},{28,16},{1,13},{... | collective-permute-start | bytes 196616 | tf_op jit(solution)/shard_map/ppermute | solution.py:45
  67.2 4.7 %collective-permute-start.38 = (bf16[32,1024]{1,0:T(8,128)(2,1)S(1)}, bf16[32,1024]{1,0:T(8,128)(2,1)S(1)}, u32[]{:S(2)}, u32[]{:S(2)}) collective-permute-start(bf16[32,1024]{1,0:T(8,128)(2,1)S(1)} %get-tuple-element.172), channel_id=1, source_target_pairs={{0,3},{1,2},{2,1},{3,0},{4,7},{5,6},{6,5},{7,4},{8,11},{9,10},{10,... | collective-permute-start | bytes 196616 | tf_op jit(solution)/shard_map/ppermute | solution.py:45
  67.3 5.8 %collective-permute-start.37 = (bf16[32,1024]{1,0:T(8,128)(2,1)S(1)}, bf16[32,1024]{1,0:T(8,128)(2,1)S(1)}, u32[]{:S(2)}, u32[]{:S(2)}) collective-permute-start(bf16[32,1024]{1,0:T(8,128)(2,1)S(1)} %get-tuple-element.173), channel_id=1, source_target_pairs={{0,2},{1,3},{2,0},{3,1},{4,6},{5,7},{6,4},{7,5},{8,10},{9,11},{10,... | collective-permute-start | bytes 196616 | tf_op jit(solution)/shard_map/ppermute | solution.py:45
  68.9 4.2 %collective-permute-start.36 = (bf16[32,1024]{1,0:T(8,128)(2,1)S(1)}, bf16[32,1024]{1,0:T(8,128)(2,1)S(1)}, u32[]{:S(2)}, u32[]{:S(2)}) collective-permute-start(bf16[32,1024]{1,0:T(8,128)(2,1)S(1)} %get-tuple-element.171), channel_id=1, source_target_pairs={{0,1},{1,0},{2,3},{3,2},{4,5},{5,4},{6,7},{7,6},{8,9},{9,8},{10,11... | collective-permute-start | bytes 196616 | tf_op jit(solution)/shard_map/ppermute | solution.py:45
  70.7 3.7 %collective-permute-start.30 = (f32[1,1024]{1,0:T(1,128)S(1)}, f32[1,1024]{1,0:T(1,128)S(1)}, u32[]{:S(2)}, u32[]{:S(2)}) collective-permute-start(f32[1,1024]{1,0:T(1,128)S(1)} %get-tuple-element.133.pool), channel_id=1, source_target_pairs={{0,2},{1,3},{2,0},{3,1},{4,6},{5,7},{6,4},{7,5},{8,10},{9,11},{10,... | collective-permute-start | bytes 12296 | tf_op jit(solution)/shard_map/ppermute | solution.py:45
  (23 other events, 148.5 us)
